TPU v7x, 256 devices: a whole 4x4x8 slice. The times are simulated.
256 devices in a mesh: ab: 16 (over z_hi, x), ij: 16 (over z_lo, y, core).
Axes of the slice: x: 4, y: 4, z: 8 (z_hi: 4, z_lo: 2; z = z_hi * 2 + z_lo), core: 2. Of those that a mesh axis runs over, the one named last changes fastest.
Arguments:
- partners: int32 [16, 9], P('ab'), may hold values from -1 to 15, as said below
- cholesky: float32 [1536, 16, 4096], P('ab', None, 'ij'), may hold values from -0.3 to 0.3
- amplitudes: float32 [16, 64], P('ij'), may hold values from -6 to 6
Outputs:
- residual: float32 [144, 16, 9216], P('ab', 'ij')
Inputs may be any that keep to these rules, and one draw needn't show every extreme that they name: partners[d, 0] = d; every unordered pair of blocks, equal ones included, stands exactly once in the whole table; the blocks in one row are distinct; -1 marks an empty slot, at most one per row and only in the last slot.
All inputs are finite; a program needn't handle non-finite values.
Results may differ from a plain program's by a relative error of at most 0.0003.
Values sent between devices are 32-bit elements; how exact they have to be, the bound alone decides.
A program may use at most 128 MiB of HBM per device.

v0:
```python
import jax
import jax.numpy as jnp
from jax import lax
from jax.sharding import PartitionSpec as P


def contract_tiles(upper, lower, amps):
    width = upper.shape[0]
    window = upper.shape[1]
    left = upper.reshape(width * window, -1)
    right = lower.reshape(width * window, -1)
    tiles = lax.dot_general(
        left,
        right,
        (((1,), (1,)), ((), ())),
        precision=lax.Precision.HIGHEST,
        preferred_element_type=jnp.float32,
    )
    tiles = tiles.reshape(width, window, width, window)
    result = jnp.einsum("acbd,icd->iab", tiles, amps, precision=lax.Precision.HIGHEST)
    return result.reshape(amps.shape[0], width * width)


def local(partners, cholesky, amplitudes):
    width = cholesky.shape[0]
    window = cholesky.shape[1] // 2
    own_index = lax.axis_index("ab")
    partner_row = partners[0]
    slots = partner_row.shape[0]
    gathered = lax.all_gather(amplitudes, "ij", axis=0, tiled=True)
    pairs_all = gathered.shape[0]
    amps = gathered.reshape(pairs_all, window, window)
    own_upper = cholesky[:, :window]
    own_lower = cholesky[:, window:]
    start_sums = jnp.zeros((slots, pairs_all, width * width), jnp.float32)
    piece = lax.all_gather(cholesky, "ab", axis=0, tiled=True)
    blocks = piece.shape[0] // width

    def visit(j, current):
        other = lax.dynamic_slice_in_dim(piece, j * width, width, 0)
        index = j * width // width
        match = partner_row == index
        present = jnp.any(match)
        position = jnp.argmax(match)

        def accumulate(running):
            is_upper = index > own_index
            upper = jnp.where(is_upper, other[:, :window], own_upper)
            lower = jnp.where(is_upper, own_lower, other[:, window:])
            return running.at[position].add(contract_tiles(upper, lower, amps))

        return lax.cond(present, accumulate, lambda running: running, current)

    partial_sums = lax.fori_loop(0, blocks, visit, start_sums)
    return lax.psum_scatter(partial_sums, "ij", scatter_dimension=1, tiled=True)


def solution(mesh):
    return jax.shard_map(
        local,
        mesh=mesh,
        in_specs=(P("ab", None), P("ab", None, "ij"), P("ij", None)),
        out_specs=P("ab", "ij", None),
        check_vma=False,
    )
```

profile of v0, /device:TPU:64, one launch (start us, length us, event | category | flops | bytes accessed | tf_op | source)
XLA Modules:
  0.0 551.0 jit_solution(17718515743921038311)
XLA Ops:
  6.5 0.7 all-gather.3.cloned.1.call-update
  7.3 20.4 %all-gather = f32[16,1,64]{2,1,0:T(1,128)S(1)} all-gather(f32[1,1,64]{2,1,0:T(1,128)} %bitcast.22), channel_id=1, replica_groups=mesh['ab'=16,'ij'=16] {'ij'}, dimensions={0}, use_global_device_ids=true | all-gather | bytes 4352 | tf_op jit(solution)/shard_map/all_gather | solution.py:30
  27.7 1.5 fusion.9
  29.3 266.9 %all-gather.3.cloned.1.call-done = f32[1536,16,256]{2,1,0:T(8,128)} async-done(((f32[96,16,256]{2,1,0:T(8,128)}), f32[1536,16,256]{2,1,0:T(8,128)}) %all-gather.3.cloned.1.call-update) | async-done | bytes 25165840 | tf_op jit(solution)/shard_map/all_gather | solution.py:36
  296.2 3.0 broadcast_in_dim.4
  299.2 152.1 %while.19 = (s32[]{:T(128)}, f32[9,16,9216]{2,1,0:T(8,128)}, s32[9]{0:T(128)S(1)}, s32[]{:T(128)}, f32[1536,16,256]{2,1,0:T(8,128)}, /*index=5*/f32[96,8,256]{2,...) while((s32[]{:T(128)}, f32[9,16,9216]{2,1,0:T(8,128)}, ...), condition=%wide.region_6.7_spmd, body=%wide.region_0.6_spmd.sunk | while | flops 1925873792 | bytes 14161398 | solution.py:54
  301.1 13.5 %conditional.2 = (f32[9,16,9216]{2,1,0:T(8,128)}) conditional(s32[]{:T(128)} %convert_element_type.11, f32[9,16,9216]{2,1,0:T(8,128)} %get-tuple-element.382, (s32[]{:T(128)}, f32[9,16,9216]{2,1,0:T(8,128)}, s32[]{:T(128)}, s32[]{:T(128)}, s32[]{:T(128)}, /*index=5*/f32[1536,16,256]{2,1,0:T(8,128)}, f32[96,8,256]{2,1,0:T(8,128)S(1)}, ...), branch_computations={%region_3.3_spmd, %region_4.5_spmd} | conditional | flops 1925873664 | bytes 14161028 | solution.py:52
  302.8 1.4 and_reduce_fusion
  304.2 1.2 dynamic-slice_select_fusion
  305.4 4.1 fusion.1
  309.6 1.8 convolution_bitcast_fusion
  312.0 2.5 fusion.5
  318.4 13.6 %conditional.2 = (f32[9,16,9216]{2,1,0:T(8,128)}) conditional(s32[]{:T(128)} %convert_element_type.11, f32[9,16,9216]{2,1,0:T(8,128)} %get-tuple-element.382, (s32[]{:T(128)}, f32[9,16,9216]{2,1,0:T(8,128)}, s32[]{:T(128)}, s32[]{:T(128)}, s32[]{:T(128)}, /*index=5*/f32[1536,16,256]{2,1,0:T(8,128)}, f32[96,8,256]{2,1,0:T(8,128)S(1)}, ...), branch_computations={%region_3.3_spmd, %region_4.5_spmd} | conditional | flops 1925873664 | bytes 14161028 | solution.py:52
  320.1 1.4 and_reduce_fusion
  321.5 1.2 dynamic-slice_select_fusion
  322.7 4.1 fusion.1
  326.9 1.8 convolution_bitcast_fusion
  329.3 2.6 fusion.5
  335.7 13.6 %conditional.2 = (f32[9,16,9216]{2,1,0:T(8,128)}) conditional(s32[]{:T(128)} %convert_element_type.11, f32[9,16,9216]{2,1,0:T(8,128)} %get-tuple-element.382, (s32[]{:T(128)}, f32[9,16,9216]{2,1,0:T(8,128)}, s32[]{:T(128)}, s32[]{:T(128)}, s32[]{:T(128)}, /*index=5*/f32[1536,16,256]{2,1,0:T(8,128)}, f32[96,8,256]{2,1,0:T(8,128)S(1)}, ...), branch_computations={%region_3.3_spmd, %region_4.5_spmd} | conditional | flops 1925873664 | bytes 14161028 | solution.py:52
  337.4 1.4 and_reduce_fusion
  338.8 1.2 dynamic-slice_select_fusion
  340.1 4.1 fusion.1
  344.2 1.8 convolution_bitcast_fusion
  346.7 2.6 fusion.5
  350.5 0.7 compare_reduce_fusion.5
  353.1 13.5 %conditional.2 = (f32[9,16,9216]{2,1,0:T(8,128)}) conditional(s32[]{:T(128)} %convert_element_type.11, f32[9,16,9216]{2,1,0:T(8,128)} %get-tuple-element.382, (s32[]{:T(128)}, f32[9,16,9216]{2,1,0:T(8,128)}, s32[]{:T(128)}, s32[]{:T(128)}, s32[]{:T(128)}, /*index=5*/f32[1536,16,256]{2,1,0:T(8,128)}, f32[96,8,256]{2,1,0:T(8,128)S(1)}, ...), branch_computations={%region_3.3_spmd, %region_4.5_spmd} | conditional | flops 1925873664 | bytes 14161028 | solution.py:52
  354.8 1.4 and_reduce_fusion
  356.2 1.2 dynamic-slice_select_fusion
  357.4 4.1 fusion.1
  361.6 1.8 convolution_bitcast_fusion
  364.0 2.5 fusion.5
  370.4 13.5 %conditional.2 = (f32[9,16,9216]{2,1,0:T(8,128)}) conditional(s32[]{:T(128)} %convert_element_type.11, f32[9,16,9216]{2,1,0:T(8,128)} %get-tuple-element.382, (s32[]{:T(128)}, f32[9,16,9216]{2,1,0:T(8,128)}, s32[]{:T(128)}, s32[]{:T(128)}, s32[]{:T(128)}, /*index=5*/f32[1536,16,256]{2,1,0:T(8,128)}, f32[96,8,256]{2,1,0:T(8,128)S(1)}, ...), branch_computations={%region_3.3_spmd, %region_4.5_spmd} | conditional | flops 1925873664 | bytes 14161028 | solution.py:52
  372.1 1.4 and_reduce_fusion
  373.5 1.2 dynamic-slice_select_fusion
  374.7 4.1 fusion.1
  378.9 1.8 convolution_bitcast_fusion
  381.3 2.6 fusion.5
  385.8 13.5 %conditional.2 = (f32[9,16,9216]{2,1,0:T(8,128)}) conditional(s32[]{:T(128)} %convert_element_type.11, f32[9,16,9216]{2,1,0:T(8,128)} %get-tuple-element.382, (s32[]{:T(128)}, f32[9,16,9216]{2,1,0:T(8,128)}, s32[]{:T(128)}, s32[]{:T(128)}, s32[]{:T(128)}, /*index=5*/f32[1536,16,256]{2,1,0:T(8,128)}, f32[96,8,256]{2,1,0:T(8,128)S(1)}, ...), branch_computations={%region_3.3_spmd, %region_4.5_spmd} | conditional | flops 1925873664 | bytes 14161028 | solution.py:52
  387.5 1.4 and_reduce_fusion
  388.9 1.2 dynamic-slice_select_fusion
  390.2 4.1 fusion.1
  394.3 1.8 convolution_bitcast_fusion
  396.7 2.6 fusion.5
  403.1 13.5 %conditional.2 = (f32[9,16,9216]{2,1,0:T(8,128)}) conditional(s32[]{:T(128)} %convert_element_type.11, f32[9,16,9216]{2,1,0:T(8,128)} %get-tuple-element.382, (s32[]{:T(128)}, f32[9,16,9216]{2,1,0:T(8,128)}, s32[]{:T(128)}, s32[]{:T(128)}, s32[]{:T(128)}, /*index=5*/f32[1536,16,256]{2,1,0:T(8,128)}, f32[96,8,256]{2,1,0:T(8,128)S(1)}, ...), branch_computations={%region_3.3_spmd, %region_4.5_spmd} | conditional | flops 1925873664 | bytes 14161028 | solution.py:52
  404.8 1.4 and_reduce_fusion
  406.2 1.2 dynamic-slice_select_fusion
  407.5 4.1 fusion.1
  411.6 1.8 convolution_bitcast_fusion
  414.0 2.5 fusion.5
  418.5 13.6 %conditional.2 = (f32[9,16,9216]{2,1,0:T(8,128)}) conditional(s32[]{:T(128)} %convert_element_type.11, f32[9,16,9216]{2,1,0:T(8,128)} %get-tuple-element.382, (s32[]{:T(128)}, f32[9,16,9216]{2,1,0:T(8,128)}, s32[]{:T(128)}, s32[]{:T(128)}, s32[]{:T(128)}, /*index=5*/f32[1536,16,256]{2,1,0:T(8,128)}, f32[96,8,256]{2,1,0:T(8,128)S(1)}, ...), branch_computations={%region_3.3_spmd, %region_4.5_spmd} | conditional | flops 1925873664 | bytes 14161028 | solution.py:52
  420.2 1.4 and_reduce_fusion
  421.6 1.2 dynamic-slice_select_fusion
  422.9 4.1 fusion.1
  427.0 1.8 convolution_bitcast_fusion
  429.4 2.6 fusion.5
  433.9 13.5 %conditional.2 = (f32[9,16,9216]{2,1,0:T(8,128)}) conditional(s32[]{:T(128)} %convert_element_type.11, f32[9,16,9216]{2,1,0:T(8,128)} %get-tuple-element.382, (s32[]{:T(128)}, f32[9,16,9216]{2,1,0:T(8,128)}, s32[]{:T(128)}, s32[]{:T(128)}, s32[]{:T(128)}, /*index=5*/f32[1536,16,256]{2,1,0:T(8,128)}, f32[96,8,256]{2,1,0:T(8,128)S(1)}, ...), branch_computations={%region_3.3_spmd, %region_4.5_spmd} | conditional | flops 1925873664 | bytes 14161028 | solution.py:52
  435.7 1.4 and_reduce_fusion
  437.1 1.2 dynamic-slice_select_fusion
  438.3 4.1 fusion.1
  442.4 1.8 convolution_bitcast_fusion
  444.9 2.6 fusion.5
  451.2 9.5 %copy.11 = f32[9,16,9216]{2,0,1:T(8,128)} copy(f32[9,16,9216]{2,1,0:T(8,128)} %get-tuple-element.291) | data formatting | bytes 10616832 | tf_op jit(solution)/shard_map/while | solution.py:54
  460.8 81.2 %reduce-scatter.2.cloned.1.call-done = f32[9,1,9216]{2,0,1:T(8,128)} async-done(((f32[9,16,9216]{2,0,1:T(8,128)}), f32[9,1,9216]{2,0,1:T(8,128)}) %reduce-scatter.2.cloned.1.call-update) | async-done | bytes 331792 | tf_op jit(solution)/shard_map/reduce_scatter | solution.py:55
  542.0 2.1 copy.12
  (62 shorter events, 26.4 us)
Async XLA Ops:
  6.5 292.6 %copy-start = (s32[1,9]{1,0:T(1,128)S(1)}, s32[1,9]{1,0:T(1,128)}, u32[]{:S(2)}) copy-start(s32[1,9]{1,0:T(1,128)} %param.9) | copy-start | bytes 112
  6.5 289.7 %all-gather.3.cloned.1.call-start = ((), (), s32[]{:S(2)}) async-start(), calls=%async_computation.1 | async-start | bytes 26738688 | tf_op jit(solution)/shard_map/all_gather | solution.py:36
  7.3 534.7 %reduce-scatter.2.cloned.1.call-start = ((), (), s32[]{:S(2)}) async-start(), calls=%async_computation.2 | async-start | bytes 10027008 | tf_op jit(solution)/shard_map/reduce_scatter | solution.py:55
Sparse Core Ops, SparseCore 0:
  9.8 286.3 all-gather.2
  460.9 81.0 reduce-scatter.1
where the time goes:
time: 554 us; the launch traced here: 551 us
  waiting for transfers between devices  349 us (63%)
  other arithmetic  67.9 us (12%)
  matrix products  53.1 us (10%)
  loops' own time  25.2 us (5%)
  local copies, waits for them, and re-layouts  22.2 us (4%)
  blocking collectives  20.4 us (4%)
  between operations  13.4 us (2%)
    all_gather x1, waiting for transfers between devices, local(): piece = lax.all_gather(cholesky, 'ab', axis=0, tiled=True)  267 us
    reduce_scatter x1, waiting for transfers between devices, local(): return lax.psum_scatter(partial_sums, 'ij', scatter_dimension=1, tiled=True)  81.2 us
    dot_general x9, matrix products, contract_tiles(): lax.dot_general(left, right, (((1,), (1,)), ((), ())), precision=lax.Prec...  37.1 us
    scatter-add x9, other arithmetic, accumulate(): return running.at[position].add(contract_tiles(upper, lower, amps))  23.1 us
    all_gather x1, blocking collectives, local(): gathered = lax.all_gather(amplitudes, 'ij', axis=0, tiled=True)  20.4 us
    dot_general x9, matrix products, contract_tiles(): jnp.einsum('acbd,icd->iab', tiles, amps, precision=lax.Precision.HIGHEST)  16 us
    another operation x16, loops' own time, visit(): return lax.cond(present, accumulate, lambda running: running, current)  15.8 us
    another operation x9, other arithmetic  12.6 us
  transfers between devices with their start and end apart: 2, of which 2 were waited for; matrix products, arithmetic and copies ran while one was open for 0% of the time, Pallas kernels for 0%

commit v1 on v0

v1 whole, which is shorter than its diff:
```python
import jax
import jax.numpy as jnp
from jax import lax
from jax.experimental import pallas as pl
from jax.experimental.pallas import tpu as pltpu
from jax.sharding import PartitionSpec as P

MESH = pl.DeviceIdType.MESH
F32 = jnp.float32
BF16 = jnp.bfloat16
VB = 96
CB = 8
QL = 256
ROWS = VB * CB
NX = 4
LT = 3
IJ = 16


def split(v):
    hi = v.astype(BF16)
    lo = (v - hi.astype(F32)).astype(BF16)
    return hi, lo


def ladder(
    partners, chol, amp, out,
    gbuf, sbuf, tbuf, left, right, tile, part, cbuf, ybuf, piece, rall,
    lsem, gs, gr, ps, pr, ts, tr, cs, cr, ys, yr, rs, rr,
):
    ab = lax.axis_index("ab")
    ij = lax.axis_index("ij")
    z, x = lax.div(ab, 4), lax.rem(ab, 4)
    zl, y, core = lax.div(ij, 8), lax.rem(lax.div(ij, 2), 4), lax.rem(ij, 2)

    def dev(z_, x_, zl_, y_, core_):
        return (z_ * 4 + x_, zl_ * 8 + y_ * 2 + core_)

    def mod4(v):
        return lax.rem(v + 8, 4)

    def gathered_half(z_):
        return jnp.where(zl == 0, jnp.where(z_ == 3, 0, 1), jnp.where(z_ == 0, 1, 0))

    sgn = 1 - 2 * zl
    gt = gathered_half(z)
    xl, xr, x2 = mod4(x - 1), mod4(x + 1), mod4(x + 2)
    yl, yr_, y2 = mod4(y - 1), mod4(y + 1), mod4(y + 2)
    zd = mod4(z - sgn)
    has2 = jnp.where(zl == 0, z < 2, z >= 2)
    forwards = jnp.logical_and(z >= 1, z <= 2)
    slot = core * 8 + y * 2 + zl

    barrier = pltpu.get_barrier_semaphore()
    peers = [(ab, lax.rem(ij + n, 16)) for n in range(1, 16)]
    for n in range(1, 4):
        for o in range(2):
            peers.append(dev(z, mod4(x + n), o, y, core))
            peers.append(dev(mod4(z + n), x, o, y, core))
    for peer in peers:
        pl.semaphore_signal(barrier, inc=1, device_id=peer, device_id_type=MESH)
    pl.semaphore_wait(barrier, len(peers))

    def remote(src, dst, send, recv, device):
        return pltpu.make_async_remote_copy(
            src_ref=src, dst_ref=dst, send_sem=send, recv_sem=recv, device_id=device, device_id_type=MESH
        )

    own_g = chol.at[:, gt]
    g_right = remote(own_g, gbuf.at[x], gs.at[0], gr.at[0], dev(z, xr, zl, y, core))
    g_left = remote(own_g, gbuf.at[x], gs.at[1], gr.at[1], dev(z, xl, zl, y, core))
    p_send = remote(
        chol.at[:, 1 - gathered_half(zd)], sbuf.at[1], ps.at[0], pr.at[0], dev(zd, x, zl, y, core)
    )
    g_right.start()
    g_left.start()
    p_send.start()
    local_g = pltpu.make_async_copy(own_g, gbuf.at[x], lsem.at[0])
    local_s = pltpu.make_async_copy(chol.at[:, 1 - gt], sbuf.at[0], lsem.at[1])
    local_g.start()
    local_s.start()
    t_sends = [
        remote(amp, tbuf.at[slot], ts.at[n - 1], tr.at[slot], (ab, lax.rem(ij + n, 16)))
        for n in range(1, 16)
    ]
    for c in t_sends:
        c.start()
    tbuf[slot] = amp[...]

    gview = gbuf.reshape(NX, VB * 2 * CB, 128)
    sview = sbuf.reshape(3, VB * 2 * CB, 128)

    def load_half(view, n, c):
        return jnp.concatenate(
            [view[n, pl.ds(h * CB + c, VB, stride=2 * CB), :] for h in range(2)], axis=1
        )

    def convert_g(n):
        base = pl.multiple_of(n * VB, 32)
        for e in range(CB):
            hi, lo = split(load_half(gview, n, e))
            right[e, pl.ds(base, VB), 0:QL] = hi
            right[e, pl.ds(base, VB), QL:2 * QL] = lo
            right[e, pl.ds(base, VB), 2 * QL:3 * QL] = hi

    def convert_s(k):
        for c in range(CB):
            hi, lo = split(load_half(sview, k, c))
            left[c * VB:(c + 1) * VB, 0:QL] = hi
            left[c * VB:(c + 1) * VB, QL:2 * QL] = hi
            left[c * VB:(c + 1) * VB, 2 * QL:3 * QL] = lo

    local_g.wait()
    local_s.wait()
    convert_g(x)
    convert_s(0)

    for n in range(1, 16):
        peer = lax.rem(ij + n, 16)
        other = lax.rem(peer, 2) * 8 + lax.rem(lax.div(peer, 2), 4) * 2 + lax.div(peer, 8)
        remote(amp, tbuf.at[other], ts.at[0], tr.at[other], (ab, peer)).wait_recv()
    tv = jnp.where(gt == 1, tbuf[:, 1, :], tbuf[:, 0, :])
    thi, tlo = split(tv)
    lane = lax.broadcasted_iota(jnp.int32, (IJ, 128), 1)
    tlo = jnp.where(lane < 64, tlo.astype(F32), 0.0).astype(BF16)
    tm = jnp.concatenate([thi, tlo], axis=0)

    remote(own_g, gbuf.at[xl], gs.at[0], gr.at[0], dev(z, xl, zl, y, core)).wait_recv()
    f_right = remote(
        gbuf.at[xl, pl.ds(0, 48)], gbuf.at[xl, pl.ds(0, 48)], gs.at[2], gr.at[2], dev(z, xr, zl, y, core)
    )
    f_right.start()
    remote(own_g, gbuf.at[xr], gs.at[1], gr.at[1], dev(z, xr, zl, y, core)).wait_recv()
    f_left = remote(
        gbuf.at[xr, pl.ds(48, 48)], gbuf.at[xr, pl.ds(48, 48)], gs.at[3], gr.at[3], dev(z, xl, zl, y, core)
    )
    f_left.start()
    p_send.wait_recv()
    p_forward = remote(sbuf.at[1], sbuf.at[2], ps.at[1], pr.at[1], dev(zd, x, zl, y, core))

    @pl.when(forwards)
    def _():
        p_forward.start()

    convert_g(xl)
    convert_g(xr)
    remote(
        gbuf.at[x2, pl.ds(0, 48)], gbuf.at[x2, pl.ds(0, 48)], gs.at[2], gr.at[2], dev(z, xl, zl, y, core)
    ).wait_recv()
    remote(
        gbuf.at[x2, pl.ds(48, 48)], gbuf.at[x2, pl.ds(48, 48)], gs.at[3], gr.at[3], dev(z, xr, zl, y, core)
    ).wait_recv()
    convert_g(x2)

    def stage1():
        def column(e, carry):
            for m in range(3):
                t = lax.dot_general(
                    left[m * 256:(m + 1) * 256, :], right[e],
                    (((1,), (1,)), ((), ())), preferred_element_type=F32,
                )
                for l in range(LT):
                    tile[e * LT + l, m * 256:(m + 1) * 256, :] = t[:, l * 128:(l + 1) * 128]
            return carry

        lax.fori_loop(0, CB, column, 0)

    def stage2(k):
        def row(n, carry):
            rhs = []
            for u in range(2):
                a = n * 2 + u
                s = jnp.concatenate(
                    [
                        jnp.concatenate(
                            [tile[e * LT + l, pl.ds(a, CB, stride=VB), :] for l in range(LT)], axis=1
                        )
                        for e in range(CB)
                    ],
                    axis=0,
                )
                hi, lo = split(s)
                rhs.append(jnp.concatenate([hi, lo], axis=0))
            r = lax.dot_general(
                tm, jnp.concatenate(rhs, axis=1), (((1,), (0,)), ((), ())), preferred_element_type=F32
            )
            r = r[:IJ] + r[IJ:]
            for u in range(2):
                for l in range(LT):
                    part[k, l, pl.ds(n * 2 + u, IJ, stride=VB), :] = r[
                        :, (u * LT + l) * 128:(u * LT + l + 1) * 128
                    ]
            return carry

        lax.fori_loop(0, VB // 2, row, 0)

    base = pl.multiple_of(core * 768, 768)
    away = pl.multiple_of((1 - core) * 768, 768)
    sibling = dev(z, x, zl, y, 1 - core)
    y_left, y_right = dev(z, x, zl, yl, core), dev(z, x, zl, yr_, core)

    def part_rows(k, y_, o):
        return part.at[k, :, pl.ds(pl.multiple_of(base + y_ * 192 + o * 96, 32), 96), :]

    def core_copy(k):
        return remote(part.at[k, :, pl.ds(away, 768), :], cbuf.at[k], cs.at[k], cr.at[k], sibling)

    def y_copies(k):
        return [
            remote(part_rows(k, y2, 0), ybuf.at[k, 0], ys.at[k, 0], yr.at[k, 0], y_right),
            remote(part_rows(k, yr_, 1), ybuf.at[k, 1], ys.at[k, 1], yr.at[k, 1], y_right),
            remote(part_rows(k, y2, 1), ybuf.at[k, 2], ys.at[k, 2], yr.at[k, 2], y_left),
            remote(part_rows(k, yl, 0), ybuf.at[k, 3], ys.at[k, 3], yr.at[k, 3], y_left),
            remote(part_rows(k, yr_, 0), ybuf.at[k, 4], ys.at[k, 4], yr.at[k, 4], y_right),
            remote(part_rows(k, yl, 1), ybuf.at[k, 5], ys.at[k, 5], yr.at[k, 5], y_left),
        ]

    def y_step1(k):
        core_copy(k).wait_recv()

        def add(n, carry):
            for l in range(LT):
                at = pl.ds(pl.multiple_of(base + n * VB, 32), VB)
                part[k, l, at, :] = part[k, l, at, :] + cbuf[k, l, pl.ds(pl.multiple_of(n * VB, 32), VB), :]
            return carry

        lax.fori_loop(0, 8, add, 0)
        for c in y_copies(k)[:4]:
            c.start()

    def merge(k, y_, o, n):
        at = pl.ds(pl.multiple_of(base + y_ * 192 + o * 96, 32), VB)
        for l in range(LT):
            part[k, l, at, :] = part[k, l, at, :] + ybuf[k, n, l]

    def y_step2(k):
        copies = y_copies(k)
        copies[0].wait_recv()
        merge(k, yr_, 0, 0)
        copies[4].start()
        copies[2].wait_recv()
        merge(k, yl, 1, 2)
        copies[5].start()

    def routes(k, op):
        zk = mod4(z + sgn * k)
        for xp in range(NX):
            valid = jnp.where(gt == 1, xp <= x, xp >= x)
            for o in range(2):
                src = piece.at[k, xp, o]

                def go(slot_, remote_ok, local_ok, device, n):
                    @pl.when(remote_ok)
                    def _():
                        c = remote(src, rall.at[zl, slot_], rs.at[k, xp, o, n], rr.at[zl, slot_], device)
                        if op == "start":
                            c.start()
                        else:
                            c.wait_send()

                    if op == "start":
                        @pl.when(local_ok)
                        def _():
                            pltpu.make_async_copy(src, rall.at[zl, slot_], rr.at[zl, slot_]).start()

                here = jnp.logical_and(xp == x, zl == o)
                if k == 0:
                    no = jnp.bool_(False)
                    go(zk * 4 + x, jnp.logical_and(valid, xp != x), no, dev(z, xp, o, y, core), 0)
                    go(
                        z * 4 + xp,
                        jnp.logical_and(valid, zl != o),
                        jnp.logical_and(valid, zl == o),
                        dev(z, x, o, y, core),
                        1,
                    )
                else:
                    go(zk * 4 + x, jnp.logical_not(here), here, dev(z, xp, o, y, core), 0)
                    go(z * 4 + xp, jnp.bool_(True), jnp.bool_(False), dev(zk, x, o, y, core), 1)

    def final(k):
        copies = y_copies(k)
        pairs = ((3, 4), (1, 5))
        for o in range(2):
            copies[pairs[o][0]].wait_recv()
            copies[pairs[o][1]].wait_recv()
            at = pl.ds(pl.multiple_of(base + y * 192 + o * 96, 32), VB)
            v = jnp.concatenate(
                [part[k, l, at, :] + ybuf[k, pairs[o][0], l] + ybuf[k, pairs[o][1], l] for l in range(LT)], axis=1
            )
            blank = jnp.zeros((VB, 128 - VB), F32)
            for xp in range(NX):
                w = v[:, xp * VB:(xp + 1) * VB]
                square = jnp.concatenate([w, blank], axis=1)
                square = jnp.concatenate([square, jnp.zeros((128 - VB, 128), F32)], axis=0)

                @pl.when(gt == 1)
                def _():
                    piece[k, xp, o] = square[:VB]

                @pl.when(gt == 0)
                def _():
                    piece[k, xp, o] = square.T[:VB]

        routes(k, "start")

    stage1()
    stage2(0)
    core_copy(0).start()
    convert_s(1)
    stage1()
    y_step1(0)
    stage2(1)
    core_copy(1).start()
    y_step2(0)

    @pl.when(has2)
    def _():
        p_forward.wait_recv()
        convert_s(2)
        stage1()

    y_step1(1)
    final(0)

    @pl.when(has2)
    def _():
        stage2(2)
        core_copy(2).start()

    y_step2(1)

    @pl.when(has2)
    def _():
        y_step1(2)

    final(1)

    @pl.when(has2)
    def _():
        y_step2(2)
        final(2)

    for s in range(2):
        for p in range(16):
            pltpu.make_async_copy(rall.at[s, p], rall.at[s, p], rr.at[s, p]).wait()
    for s in range(out.shape[0]):
        p = partners[0, s]
        at = jnp.maximum(p, 0)
        out[s] = jnp.where(p >= 0, rall[0, at] + rall[1, at], 0.0)

    for c in [g_right, g_left, p_send, f_right, f_left] + t_sends:
        c.wait_send()

    @pl.when(forwards)
    def _():
        p_forward.wait_send()

    def drain(k):
        core_copy(k).wait_send()
        for c in y_copies(k):
            c.wait_send()
        routes(k, "wait")

    drain(0)
    drain(1)

    @pl.when(has2)
    def _():
        drain(2)


def local(partners, cholesky, amplitudes):
    slots = partners.shape[1]
    chol = cholesky.reshape(VB, 2, CB, 2, 128).transpose(0, 1, 3, 2, 4)
    flat = amplitudes.reshape(1, CB * CB)
    turned = amplitudes.reshape(CB, CB).T.reshape(1, CB * CB)
    amp = jnp.concatenate(
        [jnp.tile(flat, (1, 2)), jnp.tile(turned, (1, 2)), jnp.zeros((6, 128), F32)], axis=0
    )
    dma = pltpu.SemaphoreType.DMA
    res = pl.pallas_call(
        ladder,
        out_shape=jax.ShapeDtypeStruct((slots, VB, 128), F32),
        in_specs=[
            pl.BlockSpec(memory_space=pltpu.SMEM),
            pl.BlockSpec(memory_space=pl.ANY),
            pl.BlockSpec(memory_space=pltpu.VMEM),
        ],
        out_specs=pl.BlockSpec(memory_space=pltpu.VMEM),
        scratch_shapes=[
            pltpu.VMEM((NX, VB, 2, CB, 128), F32),
            pltpu.VMEM((3, VB, 2, CB, 128), F32),
            pltpu.VMEM((IJ, 8, 128), F32),
            pltpu.VMEM((ROWS, 3 * QL), BF16),
            pltpu.VMEM((CB, NX * VB, 3 * QL), BF16),
            pltpu.VMEM((CB * LT, ROWS, 128), F32),
            pltpu.VMEM((3, LT, IJ * VB, 128), F32),
            pltpu.VMEM((3, LT, 8 * VB, 128), F32),
            pltpu.VMEM((3, 6, LT, VB, 128), F32),
            pltpu.VMEM((3, NX, 2, VB, 128), F32),
            pltpu.VMEM((2, 16, VB, 128), F32),
            dma((2,)),
            dma((4,)), dma((4,)),
            dma((2,)), dma((2,)),
            dma((15,)), dma((16,)),
            dma((3,)), dma((3,)),
            dma((3, 6)), dma((3, 6)),
            dma((3, NX, 2, 2)), dma((2, 16)),
        ],
        compiler_params=pltpu.CompilerParams(
            collective_id=0, has_side_effects=True, vmem_limit_bytes=56 * 1024 * 1024
        ),
    )(partners, chol, amp)
    return res[:, :, :VB].reshape(slots, 1, VB * VB)


def solution(mesh):
    return jax.shard_map(
        local,
        mesh=mesh,
        in_specs=(P("ab", None), P("ab", None, "ij"), P("ij", None)),
        out_specs=P("ab", "ij", None),
        check_vma=False,
    )
```

time: 554 us -> 154 us (0.28)
  the two profiles are of different devices: /device:TPU:64 before, /device:TPU:32 now
where the time goes in v1:
time: 154 us
  Pallas kernels  148 us (96%)
  local copies, waits for them, and re-layouts  3.86 us (3%)
  other arithmetic  1.99 us (1%)
    pallas_call x1, Pallas kernels, local(): pl.pallas_call(ladder, out_shape=jax.ShapeDtypeStruct((slots, VB, 128), F...  148 us

profile of v1, /device:TPU:32, one launch (start us, length us, event | category | flops | bytes accessed | tf_op | source)
XLA Modules:
  0.0 153.9 jit_solution(9284936538622233772)
XLA Ops:
  0.0 0.5 broadcast.11
  0.5 1.3 reduce.3
  1.8 0.1 pad.2.clone
  1.9 0.7 tile.22
  2.6 0.1 tile.23
  2.6 0.1 reshape.22
  2.7 0.1 copy.6
  2.8 0.1 tile.24
  2.9 0.1 tile.26
  3.0 0.7 maximum_maximum_fusion.amp
  3.6 148.1 %shard_map.37 = f32[9,96,128]{2,1,0:T(8,128)} custom-call(s32[1,9]{1,0:T(1,128)} %partners.1, f32[96,2,2,8,128]{4,3,2,1,0:T(8,128)} %bitcast.7, f32[8,128]{1,0:T(8,128)} %maximum_maximum_fusion.amp), custom_call_target="tpu_custom_call" | custom-call | tf_op jit(solution)/shard_map/pallas_call | solution.py:382
  151.7 2.2 %reshape.24 = f32[9,1,9216]{2,1,0:T(1,128)} reshape(f32[9,96,96]{2,1,0:T(8,128)} %bitcast.6) | data formatting | bytes 663552 | tf_op jit(solution)/shard_map/reshape | solution.py:415
  (2 shorter events, 0.0 us)

commit v2 on v1

v2 whole, which is shorter than its diff:
```python
import jax
import jax.numpy as jnp
from jax import lax
from jax.experimental import pallas as pl
from jax.experimental.pallas import tpu as pltpu
from jax.sharding import PartitionSpec as P

MESH = pl.DeviceIdType.MESH
F32 = jnp.float32
BF16 = jnp.bfloat16
VB = 96
CB = 8
QL = 256
ROWS = VB * CB
NX = 4
LT = 3
CH = 32
IJ = 16


def split(v):
    hi = v.astype(BF16)
    lo = (v - hi.astype(F32)).astype(BF16)
    return hi, lo


def ladder(
    partners, chol, amp, out,
    gbuf, sbuf, abuf, tbuf, wide, left, right, tile, part, cbuf, ybuf, square, piece, rall,
    lsem, gs, gr, ps, pr, ts, tr, cs, cr, ys, yr, rs, rr,
):
    ab = lax.axis_index("ab")
    ij = lax.axis_index("ij")
    z, x = lax.div(ab, 4), lax.rem(ab, 4)
    zl, y, core = lax.div(ij, 8), lax.rem(lax.div(ij, 2), 4), lax.rem(ij, 2)

    def dev(z_, x_, zl_, y_, core_):
        return (z_ * 4 + x_, zl_ * 8 + y_ * 2 + core_)

    def mod4(v):
        return lax.rem(v + 8, 4)

    def gathered_half(z_):
        return jnp.where(zl == 0, jnp.where(z_ == 3, 0, 1), jnp.where(z_ == 0, 1, 0))

    sgn = 1 - 2 * zl
    gt = gathered_half(z)
    xl, xr, x2 = mod4(x - 1), mod4(x + 1), mod4(x + 2)
    yl, yr_, y2 = mod4(y - 1), mod4(y + 1), mod4(y + 2)
    zd = mod4(z - sgn)
    has2 = jnp.where(zl == 0, z < 2, z >= 2)
    forwards = jnp.logical_and(z >= 1, z <= 2)
    slot = core * 8 + y * 2 + zl

    barrier = pltpu.get_barrier_semaphore()
    peers = [(ab, lax.rem(ij + n, 16)) for n in range(1, 16)]
    for n in range(1, 4):
        for o in range(2):
            peers.append(dev(z, mod4(x + n), o, y, core))
            peers.append(dev(mod4(z + n), x, o, y, core))
    for peer in peers:
        pl.semaphore_signal(barrier, inc=1, device_id=peer, device_id_type=MESH)
    own_g = chol.at[:, gt]
    local_g = pltpu.make_async_copy(own_g, gbuf.at[x], lsem.at[0])
    local_s = pltpu.make_async_copy(chol.at[:, 1 - gt], sbuf.at[0], lsem.at[1])
    local_g.start()
    local_s.start()
    row = jnp.concatenate([amp[...], jnp.zeros((1, 64), F32)], axis=1)
    abuf[...] = jnp.broadcast_to(row, (8, 128))
    pl.semaphore_wait(barrier, len(peers))

    def remote(src, dst, send, recv, device):
        return pltpu.make_async_remote_copy(
            src_ref=src, dst_ref=dst, send_sem=send, recv_sem=recv, device_id=device, device_id_type=MESH
        )

    to_right, to_left = dev(z, xr, zl, y, core), dev(z, xl, zl, y, core)
    to_down = dev(zd, x, zl, y, core)

    def g_chunk(j, d):
        return remote(
            chol.at[pl.ds(j * CH, CH), gt], gbuf.at[x, pl.ds(j * CH, CH)], gs.at[j, d], gr.at[j, d],
            (to_right, to_left)[d],
        )

    def g_from(j, d):
        at = gbuf.at[(xl, xr)[d], pl.ds(j * CH, CH)]
        return remote(at, at, gs.at[j, d], gr.at[j, d], (to_right, to_left)[d])

    def g_forward(j, d):
        at = gbuf.at[(xl, xr)[d], pl.ds(j * CH + d * 16, 16)]
        return remote(at, at, gs.at[j, 2 + d], gr.at[j, 2 + d], (to_right, to_left)[d])

    def g_behind(j, d):
        at = gbuf.at[x2, pl.ds(j * CH + d * 16, 16)]
        return remote(at, at, gs.at[j, 2 + d], gr.at[j, 2 + d], (to_right, to_left)[d])

    def p_chunk(m):
        return remote(
            chol.at[pl.ds(m * CH, CH), 1 - gathered_half(zd)], sbuf.at[1, pl.ds(m * CH, CH)],
            ps.at[0, m], pr.at[0, m], to_down,
        )

    def p_forward(m):
        return remote(
            sbuf.at[1, pl.ds(m * CH, CH)], sbuf.at[2, pl.ds(m * CH, CH)], ps.at[1, m], pr.at[1, m], to_down
        )

    for d in range(2):
        g_chunk(0, d).start()
    for m in range(3):
        p_chunk(m).start()
    t_sends = [
        remote(abuf, tbuf.at[slot], ts.at[n - 1], tr.at[slot], (ab, lax.rem(ij + n, 16)))
        for n in range(1, 16)
    ]
    for c in t_sends:
        c.start()
    tbuf[slot] = abuf[...]

    gview = gbuf.reshape(NX, VB * 2 * CB, 128)

    def convert_g(n, j):
        for e in range(CB):
            v = jnp.concatenate(
                [gview[n, pl.ds(j * CH * 16 + h * CB + e, CH, stride=2 * CB), :] for h in range(2)], axis=1
            )
            hi, lo = split(v)
            at = pl.ds(pl.multiple_of(e * 128 + n * CH, CH), CH)
            right[j, at, 0:QL] = hi
            right[j, at, QL:2 * QL] = lo
            right[j, at, 2 * QL:3 * QL] = hi

    def convert_s(k, m):
        for h in range(2):
            v = sbuf[k, pl.ds(m * CH, CH), h].reshape(CH * CB, 128)
            hi, lo = split(v)
            at = pl.ds(m * CH * CB, CH * CB)
            left[k, at, h * 128:h * 128 + 128] = hi
            left[k, at, QL + h * 128:QL + h * 128 + 128] = hi
            left[k, at, 2 * QL + h * 128:2 * QL + h * 128 + 128] = lo

    local_g.wait()
    local_s.wait()
    for j in range(LT):
        convert_g(x, j)
        convert_s(0, j)

    for n in range(1, 16):
        peer = lax.rem(ij + n, 16)
        other = lax.rem(peer, 2) * 8 + lax.rem(lax.div(peer, 2), 4) * 2 + lax.div(peer, 8)
        remote(abuf, tbuf.at[other], ts.at[0], tr.at[other], (ab, peer)).wait_recv()
    source = lax.broadcasted_iota(jnp.int32, (128, 512), 0)
    target = lax.rem(lax.broadcasted_iota(jnp.int32, (128, 512), 1), 64)
    turned = lax.rem(target, 8) * 8 + lax.div(target, 8)
    pick = jnp.where(source == jnp.where(gt == 1, turned, target), 1.0, 0.0).astype(BF16)
    same = lax.rem(lax.broadcasted_iota(jnp.int32, (128, 512), 0), 8) == lax.div(
        lax.broadcasted_iota(jnp.int32, (128, 512), 1), 64
    )
    for n, v in enumerate(split(tbuf[:, 0, :])):
        w = jnp.dot(v, pick, preferred_element_type=F32)
        w = jnp.broadcast_to(w[:, None, :], (IJ, 8, 512)).reshape(128, 512)
        wide[n * 128:(n + 1) * 128] = jnp.where(same, w, 0.0).astype(BF16)

    def stage1(k, j, m):
        def column(e2, carry):
            at = pl.ds(pl.multiple_of(e2 * 256, 256), 256)
            for n in range(3):
                t = lax.dot_general(
                    left[k, (n if m is None else m) * 256:((n if m is None else m) + 1) * 256, :],
                    right[n if j is None else j, at, :],
                    (((1,), (1,)), ((), ())), preferred_element_type=F32,
                )
                for u in range(2):
                    tile[e2 * 2 + u, n * 256:(n + 1) * 256, :] = t[:, u * 128:(u + 1) * 128]
            return carry

        lax.fori_loop(0, CB // 2, column, 0)

    def stage2(k, j, m):
        def rows(n, carry):
            his, los = [], []
            for u in range(2):
                base_ = (n * 2 + u) * 64
                s = jnp.concatenate(
                    [tile[e, pl.ds(pl.multiple_of(base_ + a * 8, 8), 8), :] for a in range(8) for e in range(CB)],
                    axis=0,
                )
                hi, lo = split(s)
                his.append(hi)
                los.append(lo)
            r = jnp.dot(wide[...], jnp.concatenate(his, axis=1), preferred_element_type=F32)
            q = jnp.dot(wide[0:128], jnp.concatenate(los, axis=1), preferred_element_type=F32)
            r = r[:128] + r[128:] + q
            for u in range(2):
                v = r[:, u * 128:(u + 1) * 128].reshape(IJ, 8, 128)
                item = n * 2 + u
                if m is None:
                    part[k, j, :, pl.ds(pl.multiple_of(item * 8, 8), 8), :] = v
                else:
                    at = pl.multiple_of(m * CH + lax.rem(item, 4) * 8, 8)
                    part[k, lax.div(item, 4), :, pl.ds(at, 8), :] = v
            return carry

        lax.fori_loop(0, 6, rows, 0)

    units = [(0, 0, None), (0, 1, None), (1, 0, None), (1, 1, None), (0, 2, None), (1, 2, None)]
    units += [(2, None, m) for m in range(3)]
    base, away = core * 8, (1 - core) * 8
    sibling = dev(z, x, zl, y, 1 - core)
    y_left, y_right = dev(z, x, zl, yl, core), dev(z, x, zl, yr_, core)

    def spans(n):
        k, j, m = units[n]
        if m is None:
            return k, pl.ds(j, 1), pl.ds(0, VB)
        return k, pl.ds(0, LT), pl.ds(m * CH, CH)

    def core_copy(n):
        k, l, a = spans(n)
        return remote(
            part.at[k, l, pl.ds(away, 8), a], cbuf.at[k, l, pl.ds(0, 8), a], cs.at[n], cr.at[n], sibling
        )

    def y_copies(n):
        k, l, a = spans(n)

        def one(c, y_, o, device):
            return remote(
                part.at[k, l, base + y_ * 2 + o, a], ybuf.at[k, c, l, a], ys.at[n, c], yr.at[n, c], device
            )

        return [
            one(0, y2, 0, y_right), one(1, yr_, 1, y_right), one(2, y2, 1, y_left),
            one(3, yl, 0, y_left), one(4, yr_, 0, y_right), one(5, yl, 1, y_left),
        ]

    def lanes_of(n):
        k, j, m = units[n]
        return k, ([j] if m is None else list(range(LT))), (slice(0, VB) if m is None else slice(m * CH, m * CH + CH))

    def y_step1(n):
        core_copy(n).wait_recv()
        k, ls, a = lanes_of(n)

        def add(i, carry):
            for l in ls:
                part[k, l, base + i, a, :] = part[k, l, base + i, a, :] + cbuf[k, l, i, a, :]
            return carry

        lax.fori_loop(0, 8, add, 0)
        for c in y_copies(n)[:4]:
            c.start()

    def y_step2(n):
        copies = y_copies(n)
        k, ls, a = lanes_of(n)
        for first, i, then in ((0, base + yr_ * 2, 4), (2, base + yl * 2 + 1, 5)):
            copies[first].wait_recv()
            for l in ls:
                part[k, l, i, a, :] = part[k, l, i, a, :] + ybuf[k, first, l, a, :]
            copies[then].start()

    def routes(k, op):
        zk = mod4(z + sgn * k)
        for xp in range(NX):
            valid = jnp.where(gt == 1, xp <= x, xp >= x)
            for o in range(2):
                src = piece.at[k, xp, o]

                def go(slot_, remote_ok, local_ok, device, n):
                    @pl.when(remote_ok)
                    def _():
                        c = remote(src, rall.at[zl, slot_], rs.at[k, xp, o, n], rr.at[zl, slot_], device)
                        if op == "start":
                            c.start()
                        else:
                            c.wait_send()

                    if op == "start":
                        @pl.when(local_ok)
                        def _():
                            pltpu.make_async_copy(src, rall.at[zl, slot_], rr.at[zl, slot_]).start()

                here = jnp.logical_and(xp == x, zl == o)
                if k == 0:
                    no = jnp.bool_(False)
                    go(zk * 4 + x, jnp.logical_and(valid, xp != x), no, dev(z, xp, o, y, core), 0)
                    go(
                        z * 4 + xp,
                        jnp.logical_and(valid, zl != o),
                        jnp.logical_and(valid, zl == o),
                        dev(z, x, o, y, core),
                        1,
                    )
                else:
                    go(zk * 4 + x, jnp.logical_not(here), here, dev(z, xp, o, y, core), 0)
                    go(z * 4 + xp, jnp.bool_(True), jnp.bool_(False), dev(zk, x, o, y, core), 1)

    lane = lax.broadcasted_iota(jnp.int32, (24, 128), 1)
    tall = lax.broadcasted_iota(jnp.int32, (VB, 128), 1)

    def final(k):
        pairs = ((3, 4), (1, 5))
        for n in range(len(units)):
            if units[n][0] == k:
                copies = y_copies(n)
                for c in (1, 3, 4, 5):
                    copies[c].wait_recv()
        for o in range(2):
            v = [
                part[k, l, base + y * 2 + o] + ybuf[k, pairs[o][0], l] + ybuf[k, pairs[o][1], l]
                for l in range(LT)
            ]
            for xp in range(NX):
                turn = [v[l] if l == xp else pltpu.roll(v[l], (l - xp) % 4 * 32, 1) for l in range(LT)]
                w = jnp.where(tall < 32, turn[0], jnp.where(tall < 64, turn[1], turn[2]))

                @pl.when(gt == 1)
                def _():
                    square[0:VB] = w

                @pl.when(gt == 0)
                def _():
                    square[...] = jnp.concatenate([w, jnp.zeros((128 - VB, 128), F32)], axis=0).T

                r = [square[pl.ds(n, 24, stride=4), :] for n in range(4)]
                p = piece.at[k, xp, o]
                p[pl.ds(0, 24, stride=3), :] = jnp.where(lane < 96, r[0], pltpu.roll(r[1], 96, 1))
                p[pl.ds(1, 24, stride=3), :] = jnp.where(lane < 64, pltpu.roll(r[1], 96, 1), pltpu.roll(r[2], 64, 1))
                p[pl.ds(2, 24, stride=3), :] = jnp.where(lane < 32, pltpu.roll(r[2], 64, 1), pltpu.roll(r[3], 32, 1))

        routes(k, "start")

    def begin(n):
        stage1(*units[n])

    def end(n):
        stage2(*units[n])
        core_copy(n).start()

    def gather(j):
        for d in range(2):
            g_from(j, d).wait_recv()
            g_forward(j, d).start()
            if j < 2:
                g_chunk(j + 1, d).start()
        convert_g(xl, j)
        convert_g(xr, j)

    def behind(j):
        for d in range(2):
            g_behind(j, d).wait_recv()
        convert_g(x2, j)

    gather(0)
    behind(0)
    begin(0)
    end(0)
    gather(1)
    behind(1)
    for m in range(3):
        p_chunk(m).wait_recv()

    @pl.when(forwards)
    def _():
        for m in range(3):
            p_forward(m).start()

    begin(1)
    y_step1(0)
    end(1)
    y_step2(0)
    for m in range(3):
        convert_s(1, m)
    begin(2)
    y_step1(1)
    end(2)
    y_step2(1)
    gather(2)
    begin(3)
    y_step1(2)
    end(3)
    y_step2(2)
    behind(2)
    begin(4)
    y_step1(3)
    end(4)
    y_step2(3)
    begin(5)
    y_step1(4)
    end(5)
    y_step2(4)

    @pl.when(has2)
    def _():
        for m in range(3):
            p_forward(m).wait_recv()
            convert_s(2, m)
            begin(6 + m)
            y_step1(5 + m)
            end(6 + m)
            y_step2(5 + m)
            if m < 2:
                final(m)
        y_step1(8)
        y_step2(8)
        final(2)

    @pl.when(jnp.logical_not(has2))
    def _():
        y_step1(5)
        final(0)
        y_step2(5)
        final(1)

    for s in range(2):
        for p in range(16):
            pltpu.make_async_copy(rall.at[s, p], rall.at[s, p], rr.at[s, p]).wait()
    for s in range(out.shape[0]):
        p = partners[0, s]
        at = jnp.maximum(p, 0)
        out[s] = jnp.where(p >= 0, rall[0, at] + rall[1, at], 0.0)

    for j in range(LT):
        for d in range(2):
            g_chunk(j, d).wait_send()
            g_forward(j, d).wait_send()
        p_chunk(j).wait_send()
    for c in t_sends:
        c.wait_send()

    @pl.when(forwards)
    def _():
        for m in range(3):
            p_forward(m).wait_send()

    def drain(n):
        core_copy(n).wait_send()
        for c in y_copies(n):
            c.wait_send()

    for n in range(6):
        drain(n)
    routes(0, "wait")
    routes(1, "wait")

    @pl.when(has2)
    def _():
        for n in range(6, 9):
            drain(n)
        routes(2, "wait")


def local(partners, cholesky, amplitudes):
    slots = partners.shape[1]
    chol = cholesky.reshape(VB, 2, CB, 2, 128).transpose(0, 1, 3, 2, 4)
    dma = pltpu.SemaphoreType.DMA
    res = pl.pallas_call(
        ladder,
        out_shape=jax.ShapeDtypeStruct((slots, 72, 128), F32),
        in_specs=[
            pl.BlockSpec(memory_space=pltpu.SMEM),
            pl.BlockSpec(memory_space=pl.ANY),
            pl.BlockSpec(memory_space=pltpu.VMEM),
        ],
        out_specs=pl.BlockSpec(memory_space=pltpu.VMEM),
        scratch_shapes=[
            pltpu.VMEM((NX, VB, 2, CB, 128), F32),
            pltpu.VMEM((3, VB, 2, CB, 128), F32),
            pltpu.VMEM((8, 128), F32),
            pltpu.VMEM((IJ, 8, 128), F32),
            pltpu.VMEM((256, 512), BF16),
            pltpu.VMEM((3, ROWS, 3 * QL), BF16),
            pltpu.VMEM((LT, CB * 128, 3 * QL), BF16),
            pltpu.VMEM((CB, ROWS, 128), F32),
            pltpu.VMEM((3, LT, IJ, VB, 128), F32),
            pltpu.VMEM((3, LT, 8, VB, 128), F32),
            pltpu.VMEM((3, 6, LT, VB, 128), F32),
            pltpu.VMEM((128, 128), F32),
            pltpu.VMEM((3, NX, 2, 72, 128), F32),
            pltpu.VMEM((2, 16, 72, 128), F32),
            dma((2,)),
            dma((3, 4)), dma((3, 4)),
            dma((2, 3)), dma((2, 3)),
            dma((15,)), dma((16,)),
            dma((9,)), dma((9,)),
            dma((9, 6)), dma((9, 6)),
            dma((3, NX, 2, 2)), dma((2, 16)),
        ],
        compiler_params=pltpu.CompilerParams(
            collective_id=0, has_side_effects=True, vmem_limit_bytes=56 * 1024 * 1024
        ),
    )(partners, chol, amplitudes)
    return res.reshape(slots, 1, VB * VB)


def solution(mesh):
    return jax.shard_map(
        local,
        mesh=mesh,
        in_specs=(P("ab", None), P("ab", None, "ij"), P("ij", None)),
        out_specs=P("ab", "ij", None),
        check_vma=False,
    )
```

time: 154 us -> 124 us (0.81)
  Pallas kernels: 148 us -> 122 us
  local copies, waits for them, and re-layouts: 3.86 us -> 1.72 us
  other arithmetic: 1.99 us -> 0 us
    pallas_call x1, Pallas kernels: 148 us -> 122 us  [local(): pl.pallas_call(ladder, out_shape=jax.ShapeDtypeStruct((slots, 72, 128), F...]
    reshape x2 -> x0, local copies, waits for them, and re-layouts: 2.29 us -> none  [the longest x1 2.21 us: local(): return res[:, :, :VB].reshape(slots, 1, VB * VB)]
where the time goes in v2:
time: 124 us
  Pallas kernels  122 us (98%)
  local copies, waits for them, and re-layouts  1.72 us (1%)
    pallas_call x1, Pallas kernels, local(): pl.pallas_call(ladder, out_shape=jax.ShapeDtypeStruct((slots, 72, 128), F...  122 us

profile of v2, /device:TPU:32, one launch (start us, length us, event | category | flops | bytes accessed | tf_op | source)
XLA Modules:
  0.0 124.2 jit_solution(4565821469616275236)
XLA Ops:
  0.0 122.4 %shard_map.37 = f32[9,72,128]{2,1,0:T(8,128)} custom-call(s32[1,9]{1,0:T(1,128)} %partners.1, f32[96,2,2,8,128]{4,3,2,1,0:T(8,128)} %bitcast.4, f32[1,64]{1,0:T(1,128)} %amp.1), custom_call_target="tpu_custom_call" | custom-call | tf_op jit(solution)/shard_map/pallas_call | solution.py:459
  122.4 1.7 %copy.7 = f32[9,1,9216]{2,1,0:T(1,128)} copy(f32[9,1,9216]{2,1,0:T(1,128)} %bitcast.5) | data formatting | bytes 663552

commit v3 on v2

v3 whole, which is shorter than its diff:
```python
import jax
import jax.numpy as jnp
from jax import lax
from jax.experimental import pallas as pl
from jax.experimental.pallas import tpu as pltpu
from jax.sharding import PartitionSpec as P

MESH = pl.DeviceIdType.MESH
F32 = jnp.float32
BF16 = jnp.bfloat16
VB = 96
CB = 8
QL = 256
ROWS = VB * CB
NX = 4
LT = 3
CH = 32
PC = 16
PN = 6
IJ = 16


def split(v):
    hi = v.astype(BF16)
    lo = (v - hi.astype(F32)).astype(BF16)
    return hi, lo


def ladder(
    partners, chol, amp, out,
    gbuf, sbuf, abuf, tbuf, wide, left, leftp, right, tile, part, cbuf, ybuf, zbuf, square, piece, rall,
    lsem, gs, gr, ps, pr, ts, tr, cs, cr, ys, yr, zs, zr, rs, rr,
):
    ab = lax.axis_index("ab")
    ij = lax.axis_index("ij")
    z, x = lax.div(ab, 4), lax.rem(ab, 4)
    zl, y, core = lax.div(ij, 8), lax.rem(lax.div(ij, 2), 4), lax.rem(ij, 2)

    def dev(z_, x_, zl_, y_, core_):
        return (z_ * 4 + x_, zl_ * 8 + y_ * 2 + core_)

    def mod4(v):
        return lax.rem(v + 8, 4)

    gt = jnp.where(z < 2, 1, 0)
    xl, xr, x2 = mod4(x - 1), mod4(x + 1), mod4(x + 2)
    yl, yr_, y2 = mod4(y - 1), mod4(y + 1), mod4(y + 2)
    heavy = lax.rem(z, 2) == 0
    ends = jnp.logical_or(z == 0, z == 3)
    slot = core * 8 + y * 2 + zl

    barrier = pltpu.get_barrier_semaphore()
    peers = [(ab, lax.rem(ij + n, 16)) for n in range(1, 16)]
    for n in range(1, 4):
        peers.append(dev(z, mod4(x + n), zl, y, core))
        peers.append(dev(mod4(z + n), x, zl, y, core))
    for peer in peers:
        pl.semaphore_signal(barrier, inc=1, device_id=peer, device_id_type=MESH)
    own_g = chol.at[:, gt]
    local_g = pltpu.make_async_copy(own_g, gbuf.at[x], lsem.at[0])
    local_s = pltpu.make_async_copy(chol.at[:, 1 - gt], sbuf.at[0], lsem.at[1])
    local_g.start()
    local_s.start()
    row = jnp.concatenate([amp[...], jnp.zeros((1, 64), F32)], axis=1)
    abuf[...] = jnp.broadcast_to(row, (8, 128))
    pl.semaphore_wait(barrier, len(peers))

    def remote(src, dst, send, recv, device):
        return pltpu.make_async_remote_copy(
            src_ref=src, dst_ref=dst, send_sem=send, recv_sem=recv, device_id=device, device_id_type=MESH
        )

    to_right, to_left = dev(z, xr, zl, y, core), dev(z, xl, zl, y, core)

    def g_chunk(j, d):
        return remote(
            chol.at[pl.ds(j * CH, CH), gt], gbuf.at[x, pl.ds(j * CH, CH)], gs.at[j, d], gr.at[j, d],
            (to_right, to_left)[d],
        )

    def g_from(j, d):
        at = gbuf.at[(xl, xr)[d], pl.ds(j * CH, CH)]
        return remote(at, at, gs.at[j, d], gr.at[j, d], (to_right, to_left)[d])

    def g_forward(j, d):
        at = gbuf.at[(xl, xr)[d], pl.ds(j * CH + d * 16, 16)]
        return remote(at, at, gs.at[j, 2 + d], gr.at[j, 2 + d], (to_right, to_left)[d])

    def g_behind(j, d):
        at = gbuf.at[x2, pl.ds(j * CH + d * 16, 16)]
        return remote(at, at, gs.at[j, 2 + d], gr.at[j, 2 + d], (to_right, to_left)[d])

    def p_send(m):
        rows = pl.ds(m * PC, PC)
        to = jnp.where(ends, 2, 1)
        return remote(
            chol.at[rows, 1 - lax.rem(z, 2)], sbuf.at[to, rows], ps.at[0, m], pr.at[to, m],
            dev(3 * (1 - lax.rem(z, 2)), x, zl, y, core),
        )

    def p_send_up(m):
        rows = pl.ds(m * PC, PC)
        return remote(
            chol.at[rows, 1], sbuf.at[1, rows], ps.at[1, m], pr.at[1, m], dev(2, x, zl, y, core)
        )

    def p_relay(m):
        rows = pl.ds(m * PC, PC)
        to = jnp.where(z == 0, 1, 2)
        return remote(
            sbuf.at[2, rows], sbuf.at[to, rows], ps.at[2, m], pr.at[to, m], dev(to, x, zl, y, core)
        )

    def p_wait(k, m):
        at = sbuf.at[k, pl.ds(m * PC, PC)]
        remote(at, at, ps.at[0, m], pr.at[k, m], to_right).wait_recv()

    def relay(m):
        @pl.when(ends)
        def _():
            p_wait(2, m)
            p_relay(m).start()

    for d in range(2):
        g_chunk(0, d).start()
    for m in range(PN):
        p_send(m).start()

    @pl.when(z == 1)
    def _():
        for m in range(PN):
            p_send_up(m).start()

    t_sends = [
        remote(abuf, tbuf.at[slot], ts.at[n - 1], tr.at[slot], (ab, lax.rem(ij + n, 16)))
        for n in range(1, 16)
    ]
    for c in t_sends:
        c.start()
    tbuf[slot] = abuf[...]

    gview = gbuf.reshape(NX, VB * 2 * CB, 128)

    def convert_g(n, j):
        for e in range(CB):
            v = jnp.concatenate(
                [gview[n, pl.ds(j * CH * 16 + h * CB + e, CH, stride=2 * CB), :] for h in range(2)], axis=1
            )
            hi, lo = split(v)
            at = pl.ds(pl.multiple_of(e * 128 + n * CH, CH), CH)
            right[j, at, 0:QL] = hi
            right[j, at, QL:2 * QL] = lo
            right[j, at, 2 * QL:3 * QL] = hi

    def convert_s(k, m):
        for h in range(2):
            v = sbuf[k, pl.ds(m * PC, PC), h].reshape(PC * CB, 128)
            hi, lo = split(v)
            to = left.at[pl.ds(m * PC * CB, PC * CB)] if k == 0 else leftp.at[m, pl.ds((k - 1) * PC * CB, PC * CB)]
            to[:, h * 128:h * 128 + 128] = hi
            to[:, QL + h * 128:QL + h * 128 + 128] = hi
            to[:, 2 * QL + h * 128:2 * QL + h * 128 + 128] = lo

    local_g.wait()
    local_s.wait()
    for j in range(LT):
        convert_g(x, j)
    for m in range(PN):
        convert_s(0, m)

    for n in range(1, 16):
        peer = lax.rem(ij + n, 16)
        other = lax.rem(peer, 2) * 8 + lax.rem(lax.div(peer, 2), 4) * 2 + lax.div(peer, 8)
        remote(abuf, tbuf.at[other], ts.at[0], tr.at[other], (ab, peer)).wait_recv()
    source = lax.broadcasted_iota(jnp.int32, (128, 512), 0)
    target = lax.rem(lax.broadcasted_iota(jnp.int32, (128, 512), 1), 64)
    turned = lax.rem(target, 8) * 8 + lax.div(target, 8)
    pick = jnp.where(source == jnp.where(gt == 1, turned, target), 1.0, 0.0).astype(BF16)
    same = lax.rem(lax.broadcasted_iota(jnp.int32, (128, 512), 0), 8) == lax.div(
        lax.broadcasted_iota(jnp.int32, (128, 512), 1), 64
    )
    for n, v in enumerate(split(tbuf[:, 0, :])):
        w = jnp.dot(v, pick, preferred_element_type=F32)
        w = jnp.broadcast_to(w[:, None, :], (IJ, 8, 512)).reshape(128, 512)
        wide[n * 128:(n + 1) * 128] = jnp.where(same, w, 0.0).astype(BF16)

    def stage1(n, ks):
        size = 256 if n < LT else 128 * ks

        def column(e2, carry):
            at = pl.ds(pl.multiple_of(e2 * 256, 256), 256)
            for r in range(3):
                lhs = left[r * 256:(r + 1) * 256, :] if n < LT else leftp[n - LT, 0:size, :]
                t = lax.dot_general(
                    lhs, right[n if n < LT else r, at, :],
                    (((1,), (1,)), ((), ())), preferred_element_type=F32,
                )
                for u in range(2):
                    tile[e2 * 2 + u, r * size:(r + 1) * size, :] = t[:, u * 128:(u + 1) * 128]
            return carry

        lax.fori_loop(0, CB // 2, column, 0)

    def stage2(n, ks):
        def rows(it, carry):
            his, los = [], []
            for u in range(2):
                base_ = (it * 2 + u) * 64
                s = jnp.concatenate(
                    [tile[e, pl.ds(pl.multiple_of(base_ + a * 8, 8), 8), :] for a in range(8) for e in range(CB)],
                    axis=0,
                )
                hi, lo = split(s)
                his.append(hi)
                los.append(lo)
            r = jnp.dot(wide[...], jnp.concatenate(his, axis=1), preferred_element_type=F32)
            q = jnp.dot(wide[0:128], jnp.concatenate(los, axis=1), preferred_element_type=F32)
            r = r[:128] + r[128:] + q
            for u in range(2):
                v = r[:, u * 128:(u + 1) * 128].reshape(IJ, 8, 128)
                if n < LT:
                    part[0, n, :, pl.ds(pl.multiple_of((it * 2 + u) * 8, 8), 8), :] = v
                else:
                    part[1 + lax.rem(it, ks), lax.div(it, ks), :, pl.ds((n - LT) * PC + u * 8, 8), :] = v
            return carry

        lax.fori_loop(0, 6 if n < LT else 3 * ks, rows, 0)

    base, away = core * 8, (1 - core) * 8
    sibling = dev(z, x, zl, y, 1 - core)
    y_left, y_right = dev(z, x, zl, yl, core), dev(z, x, zl, yr_, core)
    z_other = dev(z, x, 1 - zl, y, core)

    def spans(n, ks):
        if n < LT:
            return pl.ds(0, 1), pl.ds(n, 1), pl.ds(0, VB)
        return pl.ds(1, ks), pl.ds(0, LT), pl.ds((n - LT) * PC, PC)

    def blocks(n, ks):
        if n < LT:
            return [(0, n)], slice(0, VB)
        return [(k, l) for k in range(1, 1 + ks) for l in range(LT)], slice((n - LT) * PC, (n - LT) * PC + PC)

    def core_copy(n, ks):
        k, l, a = spans(n, ks)
        return remote(
            part.at[k, l, pl.ds(away, 8), a], cbuf.at[k, l, pl.ds(0, 8), a], cs.at[n], cr.at[n], sibling
        )

    def y_copies(n, ks):
        k, l, a = spans(n, ks)

        def one(c, y_, o, device):
            return remote(
                part.at[k, l, base + y_ * 2 + o, a], ybuf.at[c, k, l, a], ys.at[n, c], yr.at[n, c], device
            )

        return [
            one(0, y2, 0, y_right), one(1, yr_, 1, y_right), one(2, y2, 1, y_left),
            one(3, yl, 0, y_left), one(4, yr_, 0, y_right), one(5, yl, 1, y_left),
        ]

    def z_copy(n, ks):
        k, l, a = spans(n, ks)
        return remote(
            part.at[k, l, base + y * 2 + (1 - zl), a], zbuf.at[k, l, a], zs.at[n], zr.at[n], z_other
        )

    def y_step1(n, ks):
        core_copy(n, ks).wait_recv()
        kls, a = blocks(n, ks)

        def add(i, carry):
            for k, l in kls:
                part[k, l, base + i, a, :] = part[k, l, base + i, a, :] + cbuf[k, l, i, a, :]
            return carry

        lax.fori_loop(0, 8, add, 0)
        for c in y_copies(n, ks)[:4]:
            c.start()

    def y_step2(n, ks):
        copies = y_copies(n, ks)
        kls, a = blocks(n, ks)
        for first, i, then in ((0, base + yr_ * 2, 4), (2, base + yl * 2 + 1, 5)):
            copies[first].wait_recv()
            for k, l in kls:
                part[k, l, i, a, :] = part[k, l, i, a, :] + ybuf[first, k, l, a, :]
            copies[then].start()

    def y_step3(n, ks):
        copies = y_copies(n, ks)
        kls, a = blocks(n, ks)
        for o, pair in enumerate(((3, 4), (1, 5))):
            for c in pair:
                copies[c].wait_recv()
            i = base + y * 2 + o
            for k, l in kls:
                part[k, l, i, a, :] = part[k, l, i, a, :] + ybuf[pair[0], k, l, a, :] + ybuf[pair[1], k, l, a, :]
        z_copy(n, ks).start()

    def routes(k, op):
        if k == 0:
            zk = z
        elif k == 1:
            zk = jnp.where(z == 1, 3, jnp.where(z == 3, 2, 1))
        else:
            zk = jnp.where(z == 0, 3, 0)
        for xp in range(NX):
            src = piece.at[k, xp]
            valid = jnp.where(gt == 1, xp <= x, xp >= x) if k == 0 else jnp.bool_(True)
            here = xp == x

            def send(device, p, n):
                c = remote(src, rall.at[p], rs.at[k, xp, n], rr.at[p], device)
                if op == "start":
                    c.start()
                else:
                    c.wait_send()

            def keep(p):
                if op == "start":
                    pltpu.make_async_copy(src, rall.at[p], rr.at[p]).start()

            @pl.when(jnp.logical_and(valid, jnp.logical_not(here)))
            def _():
                send(dev(z, xp, zl, y, core), zk * 4 + x, 0)

            if k == 0:
                @pl.when(valid)
                def _():
                    keep(z * 4 + xp)
            else:
                @pl.when(here)
                def _():
                    keep(zk * 4 + x)

                send(dev(zk, x, zl, y, core), z * 4 + xp, 1)

    lane = lax.broadcasted_iota(jnp.int32, (24, 128), 1)
    tall = lax.broadcasted_iota(jnp.int32, (VB, 128), 1)

    def final(k):
        v = [part[k, l, base + y * 2 + zl] + zbuf[k, l] for l in range(LT)]
        for xp in range(NX):
            turn = [v[l] if l == xp else pltpu.roll(v[l], (l - xp) % 4 * 32, 1) for l in range(LT)]
            w = jnp.where(tall < 32, turn[0], jnp.where(tall < 64, turn[1], turn[2]))

            @pl.when(gt == 1)
            def _():
                square[0:VB] = w

            @pl.when(gt == 0)
            def _():
                square[...] = jnp.concatenate([w, jnp.zeros((128 - VB, 128), F32)], axis=0).T

            r = [square[pl.ds(n, 24, stride=4), :] for n in range(4)]
            p = piece.at[k, xp]
            p[pl.ds(0, 24, stride=3), :] = jnp.where(lane < 96, r[0], pltpu.roll(r[1], 96, 1))
            p[pl.ds(1, 24, stride=3), :] = jnp.where(lane < 64, pltpu.roll(r[1], 96, 1), pltpu.roll(r[2], 64, 1))
            p[pl.ds(2, 24, stride=3), :] = jnp.where(lane < 32, pltpu.roll(r[2], 64, 1), pltpu.roll(r[3], 32, 1))
        routes(k, "start")

    def gather(j):
        for d in range(2):
            g_from(j, d).wait_recv()
            g_forward(j, d).start()
            if j < 2:
                g_chunk(j + 1, d).start()
        convert_g(xl, j)
        convert_g(xr, j)

    def behind(j):
        for d in range(2):
            g_behind(j, d).wait_recv()
        convert_g(x2, j)

    gather(0)
    relay(0)
    behind(0)
    stage1(0, 1)
    stage2(0, 1)
    core_copy(0, 1).start()
    relay(1)
    gather(1)
    relay(2)
    behind(1)
    stage1(1, 1)
    y_step1(0, 1)
    stage2(1, 1)
    core_copy(1, 1).start()
    y_step2(0, 1)
    relay(3)
    gather(2)
    y_step1(1, 1)
    behind(2)
    stage1(2, 1)
    y_step2(1, 1)
    stage2(2, 1)
    core_copy(2, 1).start()
    y_step3(0, 1)
    relay(4)

    def rest(ks):
        for m in range(PN):
            n = LT + m
            if m == PN - 1:
                y_step1(n - 1, ks)
            for k in range(1, 1 + ks):
                if k == 1:
                    p_wait(1, m)
                else:
                    @pl.when(z == 2)
                    def _():
                        p_wait(2, m)
                convert_s(k, m)
            stage1(n, ks)
            if m < PN - 1:
                y_step1(n - 1, 1 if m == 0 else ks)
            else:
                y_step2(n - 1, ks)
            stage2(n, ks)
            core_copy(n, ks).start()
            if m == 1:
                relay(5)
            if m < PN - 1:
                y_step2(n - 1, 1 if m == 0 else ks)
            y_step3(n - 2, 1 if m < 2 else ks)
            if m == 2:
                for u in range(LT):
                    z_copy(u, 1).wait_recv()
                final(0)
        n = LT + PN - 1
        y_step1(n, ks)
        y_step3(n - 1, ks)
        y_step2(n, ks)
        y_step3(n, ks)
        for m in range(PN):
            z_copy(LT + m, ks).wait_recv()
        for k in range(1, 1 + ks):
            final(k)

    @pl.when(heavy)
    def _():
        rest(2)

    @pl.when(jnp.logical_not(heavy))
    def _():
        rest(1)

    for p in range(16):
        pltpu.make_async_copy(rall.at[p], rall.at[p], rr.at[p]).wait()
    for s in range(out.shape[0]):
        p = partners[0, s]
        out[s] = jnp.where(p >= 0, rall[jnp.maximum(p, 0)], 0.0)

    for j in range(LT):
        for d in range(2):
            g_chunk(j, d).wait_send()
            g_forward(j, d).wait_send()
    for m in range(PN):
        p_send(m).wait_send()
    for c in t_sends:
        c.wait_send()

    @pl.when(z == 1)
    def _():
        for m in range(PN):
            p_send_up(m).wait_send()

    @pl.when(ends)
    def _():
        for m in range(PN):
            p_relay(m).wait_send()

    def drain(n, ks):
        core_copy(n, ks).wait_send()
        for c in y_copies(n, ks):
            c.wait_send()
        z_copy(n, ks).wait_send()

    for n in range(LT):
        drain(n, 1)
    routes(0, "wait")
    routes(1, "wait")

    @pl.when(heavy)
    def _():
        for n in range(LT, LT + PN):
            drain(n, 2)
        routes(2, "wait")

    @pl.when(jnp.logical_not(heavy))
    def _():
        for n in range(LT, LT + PN):
            drain(n, 1)


def local(partners, cholesky, amplitudes):
    slots = partners.shape[1]
    chol = cholesky.reshape(VB, 2, CB, 2, 128).transpose(0, 1, 3, 2, 4)
    dma = pltpu.SemaphoreType.DMA
    res = pl.pallas_call(
        ladder,
        out_shape=jax.ShapeDtypeStruct((slots, 72, 128), F32),
        in_specs=[
            pl.BlockSpec(memory_space=pltpu.SMEM),
            pl.BlockSpec(memory_space=pl.ANY),
            pl.BlockSpec(memory_space=pltpu.VMEM),
        ],
        out_specs=pl.BlockSpec(memory_space=pltpu.VMEM),
        scratch_shapes=[
            pltpu.VMEM((NX, VB, 2, CB, 128), F32),
            pltpu.VMEM((3, VB, 2, CB, 128), F32),
            pltpu.VMEM((8, 128), F32),
            pltpu.VMEM((IJ, 8, 128), F32),
            pltpu.VMEM((256, 512), BF16),
            pltpu.VMEM((ROWS, 3 * QL), BF16),
            pltpu.VMEM((PN, 2 * PC * CB, 3 * QL), BF16),
            pltpu.VMEM((LT, CB * 128, 3 * QL), BF16),
            pltpu.VMEM((CB, ROWS, 128), F32),
            pltpu.VMEM((3, LT, IJ, VB, 128), F32),
            pltpu.VMEM((3, LT, 8, VB, 128), F32),
            pltpu.VMEM((6, 3, LT, VB, 128), F32),
            pltpu.VMEM((3, LT, VB, 128), F32),
            pltpu.VMEM((128, 128), F32),
            pltpu.VMEM((3, NX, 72, 128), F32),
            pltpu.VMEM((16, 72, 128), F32),
            dma((2,)),
            dma((3, 4)), dma((3, 4)),
            dma((3, PN)), dma((3, PN)),
            dma((15,)), dma((16,)),
            dma((9,)), dma((9,)),
            dma((9, 6)), dma((9, 6)),
            dma((9,)), dma((9,)),
            dma((3, NX, 2)), dma((16,)),
        ],
        compiler_params=pltpu.CompilerParams(
            collective_id=0, has_side_effects=True, vmem_limit_bytes=56 * 1024 * 1024
        ),
    )(partners, chol, amplitudes)
    return res.reshape(slots, 1, VB * VB)


def solution(mesh):
    return jax.shard_map(
        local,
        mesh=mesh,
        in_specs=(P("ab", None), P("ab", None, "ij"), P("ij", None)),
        out_specs=P("ab", "ij", None),
        check_vma=False,
    )
```

time: 124 us -> 143 us (1.15)
  the two profiles are of different devices: /device:TPU:32 before, /device:TPU:64 now
where the time goes in v3:
time: 143 us; the launch traced here: 142 us
  Pallas kernels  140 us (98%)
  local copies, waits for them, and re-layouts  1.72 us (1%)
    pallas_call x1, Pallas kernels, local(): pl.pallas_call(ladder, out_shape=jax.ShapeDtypeStruct((slots, 72, 128), F...  140 us

profile of v3, /device:TPU:64, one launch (start us, length us, event | category | flops | bytes accessed | tf_op | source)
XLA Modules:
  0.0 141.8 jit_solution(862176822142054129)
XLA Ops:
  0.0 140.1 %shard_map.37 = f32[9,72,128]{2,1,0:T(8,128)} custom-call(s32[1,9]{1,0:T(1,128)} %partners.1, f32[96,2,2,8,128]{4,3,2,1,0:T(8,128)} %bitcast.4, f32[1,64]{1,0:T(1,128)} %amp.1), custom_call_target="tpu_custom_call" | custom-call | tf_op jit(solution)/shard_map/pallas_call | solution.py:503
  140.1 1.7 %copy.7 = f32[9,1,9216]{2,1,0:T(1,128)} copy(f32[9,1,9216]{2,1,0:T(1,128)} %bitcast.5) | data formatting | bytes 663552

commit v4 on v3

--- a/solution.py
+++ b/solution.py
@@ -115,22 +115,32 @@
         at = sbuf.at[k, pl.ds(m * PC, PC)]
         remote(at, at, ps.at[0, m], pr.at[k, m], to_right).wait_recv()
 
-    def relay(m):
+    for d in range(2):
+        g_chunk(0, d).start()
+    def p_start(m):
+        p_send(m).start()
+
+        @pl.when(z == 1)
+        def _():
+            p_send_up(m).start()
+
+    def pump(m):
+        p_send(m).wait_send()
+
+        @pl.when(z == 1)
+        def _():
+            p_send_up(m).wait_send()
+
+        if m + 2 < PN:
+            p_start(m + 2)
+
         @pl.when(ends)
         def _():
             p_wait(2, m)
             p_relay(m).start()
 
-    for d in range(2):
-        g_chunk(0, d).start()
-    for m in range(PN):
-        p_send(m).start()
-
-    @pl.when(z == 1)
-    def _():
-        for m in range(PN):
-            p_send_up(m).start()
-
+    p_start(0)
+    p_start(1)
     t_sends = [
         remote(abuf, tbuf.at[slot], ts.at[n - 1], tr.at[slot], (ab, lax.rem(ij + n, 16)))
         for n in range(1, 16)
@@ -184,15 +194,22 @@
         w = jnp.broadcast_to(w[:, None, :], (IJ, 8, 512)).reshape(128, 512)
         wide[n * 128:(n + 1) * 128] = jnp.where(same, w, 0.0).astype(BF16)
 
+    units = [("own", 0), ("own", 1), ("half", 0), ("half", 1), ("own", 2), ("half", 2)]
+    units += [("rows", m) for m in range(3, PN)]
+
     def stage1(n, ks):
-        size = 256 if n < LT else 128 * ks
+        kind, v = units[n]
+        size = 256 if kind == "own" else 128 * ks
 
         def column(e2, carry):
             at = pl.ds(pl.multiple_of(e2 * 256, 256), 256)
             for r in range(3):
-                lhs = left[r * 256:(r + 1) * 256, :] if n < LT else leftp[n - LT, 0:size, :]
+                if kind == "own":
+                    lhs = left[r * 256:(r + 1) * 256, :]
+                else:
+                    lhs = leftp[r if kind == "half" else v, 0:size, :]
                 t = lax.dot_general(
-                    lhs, right[n if n < LT else r, at, :],
+                    lhs, right[r if kind == "rows" else v, at, :],
                     (((1,), (1,)), ((), ())), preferred_element_type=F32,
                 )
                 for u in range(2):
@@ -202,6 +219,8 @@
         lax.fori_loop(0, CB // 2, column, 0)
 
     def stage2(n, ks):
+        kind, w = units[n]
+
         def rows(it, carry):
             his, los = [], []
             for u in range(2):
@@ -218,28 +237,34 @@
             r = r[:128] + r[128:] + q
             for u in range(2):
                 v = r[:, u * 128:(u + 1) * 128].reshape(IJ, 8, 128)
-                if n < LT:
-                    part[0, n, :, pl.ds(pl.multiple_of((it * 2 + u) * 8, 8), 8), :] = v
+                if kind == "own":
+                    part[0, w, :, pl.ds(pl.multiple_of((it * 2 + u) * 8, 8), 8), :] = v
+                elif kind == "half":
+                    at = pl.multiple_of(lax.div(it, ks) * PC + u * 8, 8)
+                    part[1 + lax.rem(it, ks), w, :, pl.ds(at, 8), :] = v
                 else:
-                    part[1 + lax.rem(it, ks), lax.div(it, ks), :, pl.ds((n - LT) * PC + u * 8, 8), :] = v
+                    part[1 + lax.rem(it, ks), lax.div(it, ks), :, pl.ds(w * PC + u * 8, 8), :] = v
             return carry
 
-        lax.fori_loop(0, 6 if n < LT else 3 * ks, rows, 0)
+        lax.fori_loop(0, 6 if kind == "own" else 3 * ks, rows, 0)
 
     base, away = core * 8, (1 - core) * 8
     sibling = dev(z, x, zl, y, 1 - core)
     y_left, y_right = dev(z, x, zl, yl, core), dev(z, x, zl, yr_, core)
     z_other = dev(z, x, 1 - zl, y, core)
 
+    def reach(n):
+        kind, v = units[n]
+        return {"own": (v, 1, 0, VB), "half": (v, 1, 0, 3 * PC), "rows": (0, LT, v * PC, PC)}[kind]
+
     def spans(n, ks):
-        if n < LT:
-            return pl.ds(0, 1), pl.ds(n, 1), pl.ds(0, VB)
-        return pl.ds(1, ks), pl.ds(0, LT), pl.ds((n - LT) * PC, PC)
+        l, ln, a, an = reach(n)
+        return pl.ds(0, 1) if units[n][0] == "own" else pl.ds(1, ks), pl.ds(l, ln), pl.ds(a, an)
 
     def blocks(n, ks):
-        if n < LT:
-            return [(0, n)], slice(0, VB)
-        return [(k, l) for k in range(1, 1 + ks) for l in range(LT)], slice((n - LT) * PC, (n - LT) * PC + PC)
+        l, ln, a, an = reach(n)
+        ks_ = [0] if units[n][0] == "own" else range(1, 1 + ks)
+        return [(k, l_) for k in ks_ for l_ in range(l, l + ln)], slice(a, a + an)
 
     def core_copy(n, ks):
         k, l, a = spans(n, ks)
@@ -376,67 +401,70 @@
         convert_g(x2, j)
 
     gather(0)
-    relay(0)
+    pump(0)
     behind(0)
     stage1(0, 1)
     stage2(0, 1)
     core_copy(0, 1).start()
-    relay(1)
+    pump(1)
+    y_step1(0, 1)
     gather(1)
-    relay(2)
+    y_step2(0, 1)
     behind(1)
+    pump(2)
     stage1(1, 1)
-    y_step1(0, 1)
     stage2(1, 1)
     core_copy(1, 1).start()
-    y_step2(0, 1)
-    relay(3)
-    gather(2)
-    y_step1(1, 1)
-    behind(2)
-    stage1(2, 1)
-    y_step2(1, 1)
-    stage2(2, 1)
-    core_copy(2, 1).start()
     y_step3(0, 1)
-    relay(4)
+
+    def fetch(ks, m):
+        for k in range(1, 1 + ks):
+            if k == 1:
+                p_wait(1, m)
+            else:
+                @pl.when(z == 2)
+                def _():
+                    p_wait(2, m)
+            convert_s(k, m)
 
     def rest(ks):
-        for m in range(PN):
-            n = LT + m
-            if m == PN - 1:
+        gather(2)
+        y_step1(1, 1)
+        pump(3)
+        for m in range(3):
+            fetch(ks, m)
+        last = len(units) - 1
+        for n in range(2, last + 1):
+            if n == last:
+                y_step2(n - 2, ks)
                 y_step1(n - 1, ks)
-            for k in range(1, 1 + ks):
-                if k == 1:
-                    p_wait(1, m)
-                else:
-                    @pl.when(z == 2)
-                    def _():
-                        p_wait(2, m)
-                convert_s(k, m)
+            if units[n][0] == "rows":
+                fetch(ks, units[n][1])
             stage1(n, ks)
-            if m < PN - 1:
-                y_step1(n - 1, 1 if m == 0 else ks)
-            else:
-                y_step2(n - 1, ks)
+            if 2 < n < last:
+                y_step2(n - 2, ks)
+                y_step1(n - 1, ks)
             stage2(n, ks)
             core_copy(n, ks).start()
-            if m == 1:
-                relay(5)
-            if m < PN - 1:
-                y_step2(n - 1, 1 if m == 0 else ks)
-            y_step3(n - 2, 1 if m < 2 else ks)
-            if m == 2:
-                for u in range(LT):
-                    z_copy(u, 1).wait_recv()
-                final(0)
-        n = LT + PN - 1
-        y_step1(n, ks)
-        y_step3(n - 1, ks)
-        y_step2(n, ks)
-        y_step3(n, ks)
-        for m in range(PN):
-            z_copy(LT + m, ks).wait_recv()
+            if n > 3:
+                y_step3(n - 3, ks)
+            if n == 3:
+                behind(2)
+                pump(4)
+            if n == 6:
+                pump(5)
+        y_step2(last - 1, ks)
+        y_step1(last, ks)
+        y_step3(last - 2, ks)
+        for u in (0, 1, 4):
+            z_copy(u, ks).wait_recv()
+        final(0)
+        y_step3(last - 1, ks)
+        y_step2(last, ks)
+        y_step3(last, ks)
+        for n in range(2, last + 1):
+            if n != 4:
+                z_copy(n, ks).wait_recv()
         for k in range(1, 1 + ks):
             final(k)
 
@@ -458,15 +486,8 @@
         for d in range(2):
             g_chunk(j, d).wait_send()
             g_forward(j, d).wait_send()
-    for m in range(PN):
-        p_send(m).wait_send()
     for c in t_sends:
         c.wait_send()
-
-    @pl.when(z == 1)
-    def _():
-        for m in range(PN):
-            p_send_up(m).wait_send()
 
     @pl.when(ends)
     def _():
@@ -479,20 +500,18 @@
             c.wait_send()
         z_copy(n, ks).wait_send()
 
-    for n in range(LT):
-        drain(n, 1)
     routes(0, "wait")
     routes(1, "wait")
 
     @pl.when(heavy)
     def _():
-        for n in range(LT, LT + PN):
+        for n in range(len(units)):
             drain(n, 2)
         routes(2, "wait")
 
     @pl.when(jnp.logical_not(heavy))
     def _():
-        for n in range(LT, LT + PN):
+        for n in range(len(units)):
             drain(n, 1)
 
 

time: 143 us -> 108 us (0.76)
  Pallas kernels: 140 us -> 106 us
    pallas_call x1, Pallas kernels: 140 us -> 106 us  [local(): pl.pallas_call(ladder, out_shape=jax.ShapeDtypeStruct((slots, 72, 128), F...]
where the time goes in v4:
time: 108 us
  Pallas kernels  106 us (98%)
  local copies, waits for them, and re-layouts  1.72 us (2%)
    pallas_call x1, Pallas kernels, local(): pl.pallas_call(ladder, out_shape=jax.ShapeDtypeStruct((slots, 72, 128), F...  106 us

profile of v4, /device:TPU:64, one launch (start us, length us, event | category | flops | bytes accessed | tf_op | source)
XLA Modules:
  0.0 107.6 jit_solution(7538122987023220834)
XLA Ops:
  0.0 105.9 %shard_map.37 = f32[9,72,128]{2,1,0:T(8,128)} custom-call(s32[1,9]{1,0:T(1,128)} %partners.1, f32[96,2,2,8,128]{4,3,2,1,0:T(8,128)} %bitcast.4, f32[1,64]{1,0:T(1,128)} %amp.1), custom_call_target="tpu_custom_call" | custom-call | tf_op jit(solution)/shard_map/pallas_call | solution.py:522
  105.9 1.7 %copy.7 = f32[9,1,9216]{2,1,0:T(1,128)} copy(f32[9,1,9216]{2,1,0:T(1,128)} %bitcast.5) | data formatting | bytes 663552

commit v5 on v4

--- a/solution.py
+++ b/solution.py
@@ -183,12 +183,10 @@
         other = lax.rem(peer, 2) * 8 + lax.rem(lax.div(peer, 2), 4) * 2 + lax.div(peer, 8)
         remote(abuf, tbuf.at[other], ts.at[0], tr.at[other], (ab, peer)).wait_recv()
     source = lax.broadcasted_iota(jnp.int32, (128, 512), 0)
-    target = lax.rem(lax.broadcasted_iota(jnp.int32, (128, 512), 1), 64)
-    turned = lax.rem(target, 8) * 8 + lax.div(target, 8)
-    pick = jnp.where(source == jnp.where(gt == 1, turned, target), 1.0, 0.0).astype(BF16)
-    same = lax.rem(lax.broadcasted_iota(jnp.int32, (128, 512), 0), 8) == lax.div(
-        lax.broadcasted_iota(jnp.int32, (128, 512), 1), 64
-    )
+    target = lax.broadcasted_iota(jnp.int32, (128, 512), 1)
+    outer, inner = lax.div(target, 64), lax.rem(target, 8)
+    pick = jnp.where(source == jnp.where(gt == 1, inner * 8 + outer, outer * 8 + inner), 1.0, 0.0).astype(BF16)
+    same = lax.rem(source, 8) == lax.rem(lax.div(target, 8), 8)
     for n, v in enumerate(split(tbuf[:, 0, :])):
         w = jnp.dot(v, pick, preferred_element_type=F32)
         w = jnp.broadcast_to(w[:, None, :], (IJ, 8, 512)).reshape(128, 512)
@@ -201,8 +199,8 @@
         kind, v = units[n]
         size = 256 if kind == "own" else 128 * ks
 
-        def column(e2, carry):
-            at = pl.ds(pl.multiple_of(e2 * 256, 256), 256)
+        def column(en, carry):
+            at = pl.ds(en * 256, 256) if isinstance(en, int) else pl.ds(pl.multiple_of(en * 256, 256), 256)
             for r in range(3):
                 if kind == "own":
                     lhs = left[r * 256:(r + 1) * 256, :]
@@ -212,41 +210,44 @@
                     lhs, right[r if kind == "rows" else v, at, :],
                     (((1,), (1,)), ((), ())), preferred_element_type=F32,
                 )
-                for u in range(2):
-                    tile[e2 * 2 + u, r * size:(r + 1) * size, :] = t[:, u * 128:(u + 1) * 128]
+                hi, lo = split(t)
+                for u in range(256 // 128):
+                    tile[0, en * 2 + u, r * size:(r + 1) * size, :] = hi[:, u * 128:(u + 1) * 128]
+                    tile[1, en * 2 + u, r * size:(r + 1) * size, :] = lo[:, u * 128:(u + 1) * 128]
             return carry
 
-        lax.fori_loop(0, CB // 2, column, 0)
+        for en in range(CB * 128 // 256):
+            column(en, 0)
 
     def stage2(n, ks):
         kind, w = units[n]
 
+        many = 4 if kind == "own" else 2 * ks
+
         def rows(it, carry):
-            his, los = [], []
-            for u in range(2):
-                base_ = (it * 2 + u) * 64
-                s = jnp.concatenate(
-                    [tile[e, pl.ds(pl.multiple_of(base_ + a * 8, 8), 8), :] for a in range(8) for e in range(CB)],
-                    axis=0,
+            cols = []
+            for h in range(2):
+                at = [(it * many + u) * 64 for u in range(many)]
+                cols.append(
+                    jnp.concatenate(
+                        [jnp.concatenate([tile[h, e, pl.ds(b, 64), :] for e in range(CB)], axis=0) for b in at], axis=1
+                    )
                 )
-                hi, lo = split(s)
-                his.append(hi)
-                los.append(lo)
-            r = jnp.dot(wide[...], jnp.concatenate(his, axis=1), preferred_element_type=F32)
-            q = jnp.dot(wide[0:128], jnp.concatenate(los, axis=1), preferred_element_type=F32)
+            r = jnp.dot(wide[...], cols[0], preferred_element_type=F32)
+            q = jnp.dot(wide[0:128], cols[1], preferred_element_type=F32)
             r = r[:128] + r[128:] + q
-            for u in range(2):
+            for u in range(many):
                 v = r[:, u * 128:(u + 1) * 128].reshape(IJ, 8, 128)
                 if kind == "own":
-                    part[0, w, :, pl.ds(pl.multiple_of((it * 2 + u) * 8, 8), 8), :] = v
+                    part[0, w, :, pl.ds((it * many + u) * 8, 8), :] = v
                 elif kind == "half":
-                    at = pl.multiple_of(lax.div(it, ks) * PC + u * 8, 8)
-                    part[1 + lax.rem(it, ks), w, :, pl.ds(at, 8), :] = v
+                    part[1 + u // 2, w, :, pl.ds(it * PC + u % 2 * 8, 8), :] = v
                 else:
-                    part[1 + lax.rem(it, ks), lax.div(it, ks), :, pl.ds(w * PC + u * 8, 8), :] = v
+                    part[1 + u // 2, it, :, pl.ds(w * PC + u % 2 * 8, 8), :] = v
             return carry
 
-        lax.fori_loop(0, 6 if kind == "own" else 3 * ks, rows, 0)
+        for it in range(3):
+            rows(it, 0)
 
     base, away = core * 8, (1 - core) * 8
     sibling = dev(z, x, zl, y, 1 - core)
@@ -428,26 +429,34 @@
             convert_s(k, m)
 
     def rest(ks):
-        gather(2)
         y_step1(1, 1)
-        pump(3)
+
+        @pl.when(jnp.logical_not(ends))
+        def _():
+            gather(2)
+
         for m in range(3):
             fetch(ks, m)
         last = len(units) - 1
         for n in range(2, last + 1):
             if n == last:
+                y_step1(n - 1, ks)
                 y_step2(n - 2, ks)
-                y_step1(n - 1, ks)
             if units[n][0] == "rows":
                 fetch(ks, units[n][1])
             stage1(n, ks)
             if 2 < n < last:
+                y_step1(n - 1, ks)
                 y_step2(n - 2, ks)
-                y_step1(n - 1, ks)
             stage2(n, ks)
             core_copy(n, ks).start()
             if n > 3:
                 y_step3(n - 3, ks)
+            if n == 2:
+                @pl.when(ends)
+                def _():
+                    gather(2)
+                pump(3)
             if n == 3:
                 behind(2)
                 pump(4)
@@ -537,7 +546,7 @@
             pltpu.VMEM((ROWS, 3 * QL), BF16),
             pltpu.VMEM((PN, 2 * PC * CB, 3 * QL), BF16),
             pltpu.VMEM((LT, CB * 128, 3 * QL), BF16),
-            pltpu.VMEM((CB, ROWS, 128), F32),
+            pltpu.VMEM((2, CB, ROWS, 128), BF16),
             pltpu.VMEM((3, LT, IJ, VB, 128), F32),
             pltpu.VMEM((3, LT, 8, VB, 128), F32),
             pltpu.VMEM((6, 3, LT, VB, 128), F32),

time: 108 us -> 99.6 us (0.922)
  Pallas kernels: 106 us -> 96.5 us
    pallas_call x1, Pallas kernels: 106 us -> 96.5 us  [local(): pl.pallas_call(ladder, out_shape=jax.ShapeDtypeStruct((slots, 72, 128), F...]
where the time goes in v5:
time: 99.6 us; the launch traced here: 98.3 us
  Pallas kernels  96.5 us (97%)
  local copies, waits for them, and re-layouts  1.72 us (2%)
    pallas_call x1, Pallas kernels, local(): pl.pallas_call(ladder, out_shape=jax.ShapeDtypeStruct((slots, 72, 128), F...  96.5 us

profile of v5, /device:TPU:64, one launch (start us, length us, event | category | flops | bytes accessed | tf_op | source)
XLA Modules:
  0.0 98.3 jit_solution(11018067287594270403)
XLA Ops:
  0.0 96.5 %shard_map.37 = f32[9,72,128]{2,1,0:T(8,128)} custom-call(s32[1,9]{1,0:T(1,128)} %partners.1, f32[96,2,2,8,128]{4,3,2,1,0:T(8,128)} %bitcast.4, f32[1,64]{1,0:T(1,128)} %amp.1), custom_call_target="tpu_custom_call" | custom-call | tf_op jit(solution)/shard_map/pallas_call | solution.py:531
  96.5 1.7 %copy.7 = f32[9,1,9216]{2,1,0:T(1,128)} copy(f32[9,1,9216]{2,1,0:T(1,128)} %bitcast.5) | data formatting | bytes 663552

commit v6 on v5

--- a/solution.py
+++ b/solution.py
@@ -47,11 +47,11 @@
     yl, yr_, y2 = mod4(y - 1), mod4(y + 1), mod4(y + 2)
     heavy = lax.rem(z, 2) == 0
     ends = jnp.logical_or(z == 0, z == 3)
-    slot = core * 8 + y * 2 + zl
 
     barrier = pltpu.get_barrier_semaphore()
-    peers = [(ab, lax.rem(ij + n, 16)) for n in range(1, 16)]
+    peers = [dev(z, x, zl, y, 1 - core), dev(z, x, 1 - zl, y, core)]
     for n in range(1, 4):
+        peers.append(dev(z, x, zl, mod4(y + n), core))
         peers.append(dev(z, mod4(x + n), zl, y, core))
         peers.append(dev(mod4(z + n), x, zl, y, core))
     for peer in peers:
@@ -141,13 +141,17 @@
 
     p_start(0)
     p_start(1)
-    t_sends = [
-        remote(abuf, tbuf.at[slot], ts.at[n - 1], tr.at[slot], (ab, lax.rem(ij + n, 16)))
-        for n in range(1, 16)
-    ]
-    for c in t_sends:
-        c.start()
-    tbuf[slot] = abuf[...]
+    def t_copy(n, send):
+        if n == 0:
+            at, device = tbuf.at[core if send else 1 - core, y, zl], dev(z, x, zl, y, 1 - core)
+        elif n == 1:
+            at, device = tbuf.at[:, y, zl if send else 1 - zl], dev(z, x, 1 - zl, y, core)
+        else:
+            at, device = tbuf.at[:, y if send else mod4(y - n + 1)], dev(z, x, zl, mod4(y + n - 1), core)
+        return remote(at, at, ts.at[n], tr.at[n], device)
+
+    tbuf[core, y, zl] = abuf[...]
+    t_copy(0, True).start()
 
     gview = gbuf.reshape(NX, VB * 2 * CB, 128)
 
@@ -178,16 +182,18 @@
     for m in range(PN):
         convert_s(0, m)
 
-    for n in range(1, 16):
-        peer = lax.rem(ij + n, 16)
-        other = lax.rem(peer, 2) * 8 + lax.rem(lax.div(peer, 2), 4) * 2 + lax.div(peer, 8)
-        remote(abuf, tbuf.at[other], ts.at[0], tr.at[other], (ab, peer)).wait_recv()
+    for n in range(2):
+        t_copy(n, False).wait_recv()
+        for o in ((1,), (2, 3, 4))[n]:
+            t_copy(o, True).start()
+    for n in range(2, 5):
+        t_copy(n, False).wait_recv()
     source = lax.broadcasted_iota(jnp.int32, (128, 512), 0)
     target = lax.broadcasted_iota(jnp.int32, (128, 512), 1)
     outer, inner = lax.div(target, 64), lax.rem(target, 8)
     pick = jnp.where(source == jnp.where(gt == 1, inner * 8 + outer, outer * 8 + inner), 1.0, 0.0).astype(BF16)
     same = lax.rem(source, 8) == lax.rem(lax.div(target, 8), 8)
-    for n, v in enumerate(split(tbuf[:, 0, :])):
+    for n, v in enumerate(split(tbuf.reshape(IJ, 8, 128)[:, 0, :])):
         w = jnp.dot(v, pick, preferred_element_type=F32)
         w = jnp.broadcast_to(w[:, None, :], (IJ, 8, 512)).reshape(128, 512)
         wide[n * 128:(n + 1) * 128] = jnp.where(same, w, 0.0).astype(BF16)
@@ -325,7 +331,7 @@
                 part[k, l, i, a, :] = part[k, l, i, a, :] + ybuf[pair[0], k, l, a, :] + ybuf[pair[1], k, l, a, :]
         z_copy(n, ks).start()
 
-    def routes(k, op):
+    def routes(k, h, op):
         if k == 0:
             zk = z
         elif k == 1:
@@ -333,12 +339,12 @@
         else:
             zk = jnp.where(z == 0, 3, 0)
         for xp in range(NX):
-            src = piece.at[k, xp]
+            src = piece.at[k, xp, h]
             valid = jnp.where(gt == 1, xp <= x, xp >= x) if k == 0 else jnp.bool_(True)
             here = xp == x
 
             def send(device, p, n):
-                c = remote(src, rall.at[p], rs.at[k, xp, n], rr.at[p], device)
+                c = remote(src, rall.at[p, h], rs.at[k, xp, h, n], rr.at[p, h], device)
                 if op == "start":
                     c.start()
                 else:
@@ -346,7 +352,7 @@
 
             def keep(p):
                 if op == "start":
-                    pltpu.make_async_copy(src, rall.at[p], rr.at[p]).start()
+                    pltpu.make_async_copy(src, rall.at[p, h], rr.at[p, h]).start()
 
             @pl.when(jnp.logical_and(valid, jnp.logical_not(here)))
             def _():
@@ -363,29 +369,46 @@
 
                 send(dev(zk, x, zl, y, core), z * 4 + xp, 1)
 
-    lane = lax.broadcasted_iota(jnp.int32, (24, 128), 1)
-    tall = lax.broadcasted_iota(jnp.int32, (VB, 128), 1)
-
-    def final(k):
-        v = [part[k, l, base + y * 2 + zl] + zbuf[k, l] for l in range(LT)]
+    lane = lax.broadcasted_iota(jnp.int32, (12, 128), 1)
+
+    def pack(k, xp, h, first):
+        r = [square[pl.ds(first + n, 12, stride=4), :] for n in range(4)]
+        p = piece.at[k, xp, h]
+        p[pl.ds(0, 12, stride=3), :] = jnp.where(lane < 96, r[0], pltpu.roll(r[1], 96, 1))
+        p[pl.ds(1, 12, stride=3), :] = jnp.where(lane < 64, pltpu.roll(r[1], 96, 1), pltpu.roll(r[2], 64, 1))
+        p[pl.ds(2, 12, stride=3), :] = jnp.where(lane < 32, pltpu.roll(r[2], 64, 1), pltpu.roll(r[3], 32, 1))
+
+    def block(k, xp, a, an):
+        v = [part[k, l, base + y * 2 + zl, a:a + an] + zbuf[k, l, a:a + an] for l in range(LT)]
+        turn = [v[l] if l == xp else pltpu.roll(v[l], (l - xp) % 4 * 32, 1) for l in range(LT)]
+        tall = lax.broadcasted_iota(jnp.int32, (an, 128), 1)
+        return jnp.where(tall < 32, turn[0], jnp.where(tall < 64, turn[1], turn[2]))
+
+    def final_half(k, h):
         for xp in range(NX):
-            turn = [v[l] if l == xp else pltpu.roll(v[l], (l - xp) % 4 * 32, 1) for l in range(LT)]
-            w = jnp.where(tall < 32, turn[0], jnp.where(tall < 64, turn[1], turn[2]))
-
-            @pl.when(gt == 1)
-            def _():
-                square[0:VB] = w
-
+            square[0:48] = block(k, xp, h * 48, 48)
+            pack(k, xp, h, 0)
+        routes(k, h, "start")
+
+    def final_turned(k):
+        for xp in range(NX):
+            w = block(k, xp, 0, VB)
+            square[...] = jnp.concatenate([w, jnp.zeros((128 - VB, 128), F32)], axis=0).T
+            for h in range(2):
+                pack(k, xp, h, h * 48)
+        for h in range(2):
+            routes(k, h, "start")
+
+    def final(k, hs):
+        @pl.when(gt == 1)
+        def _():
+            for h in hs:
+                final_half(k, h)
+
+        if 1 in hs:
             @pl.when(gt == 0)
             def _():
-                square[...] = jnp.concatenate([w, jnp.zeros((128 - VB, 128), F32)], axis=0).T
-
-            r = [square[pl.ds(n, 24, stride=4), :] for n in range(4)]
-            p = piece.at[k, xp]
-            p[pl.ds(0, 24, stride=3), :] = jnp.where(lane < 96, r[0], pltpu.roll(r[1], 96, 1))
-            p[pl.ds(1, 24, stride=3), :] = jnp.where(lane < 64, pltpu.roll(r[1], 96, 1), pltpu.roll(r[2], 64, 1))
-            p[pl.ds(2, 24, stride=3), :] = jnp.where(lane < 32, pltpu.roll(r[2], 64, 1), pltpu.roll(r[3], 32, 1))
-        routes(k, "start")
+                final_turned(k)
 
     def gather(j):
         for d in range(2):
@@ -446,36 +469,46 @@
                 fetch(ks, units[n][1])
             stage1(n, ks)
             if 2 < n < last:
-                y_step1(n - 1, ks)
+                if n == 4:
+                    @pl.when(jnp.logical_not(ends))
+                    def _():
+                        y_step1(3, ks)
+                else:
+                    y_step1(n - 1, ks)
                 y_step2(n - 2, ks)
             stage2(n, ks)
             core_copy(n, ks).start()
             if n > 3:
                 y_step3(n - 3, ks)
-            if n == 2:
+            if n == 3:
                 @pl.when(ends)
                 def _():
+                    y_step1(3, ks)
                     gather(2)
+
                 pump(3)
-            if n == 3:
                 behind(2)
+            if n == 4:
                 pump(4)
             if n == 6:
                 pump(5)
         y_step2(last - 1, ks)
         y_step1(last, ks)
-        y_step3(last - 2, ks)
         for u in (0, 1, 4):
             z_copy(u, ks).wait_recv()
-        final(0)
+        final(0, (0, 1))
+        y_step3(last - 2, ks)
+        for u in (2, 3, 5):
+            z_copy(u, ks).wait_recv()
+        for k in range(ks, 0, -1):
+            final(k, (0,))
         y_step3(last - 1, ks)
         y_step2(last, ks)
         y_step3(last, ks)
-        for n in range(2, last + 1):
-            if n != 4:
-                z_copy(n, ks).wait_recv()
-        for k in range(1, 1 + ks):
-            final(k)
+        for u in (6, 7, 8):
+            z_copy(u, ks).wait_recv()
+        for k in range(ks, 0, -1):
+            final(k, (1,))
 
     @pl.when(heavy)
     def _():
@@ -486,17 +519,19 @@
         rest(1)
 
     for p in range(16):
-        pltpu.make_async_copy(rall.at[p], rall.at[p], rr.at[p]).wait()
+        for h in range(2):
+            pltpu.make_async_copy(rall.at[p, h], rall.at[p, h], rr.at[p, h]).wait()
     for s in range(out.shape[0]):
         p = partners[0, s]
-        out[s] = jnp.where(p >= 0, rall[jnp.maximum(p, 0)], 0.0)
+        for h in range(2):
+            out[s, h * 36:h * 36 + 36] = jnp.where(p >= 0, rall[jnp.maximum(p, 0), h, 0:36], 0.0)
 
     for j in range(LT):
         for d in range(2):
             g_chunk(j, d).wait_send()
             g_forward(j, d).wait_send()
-    for c in t_sends:
-        c.wait_send()
+    for n in range(5):
+        t_copy(n, True).wait_send()
 
     @pl.when(ends)
     def _():
@@ -509,14 +544,18 @@
             c.wait_send()
         z_copy(n, ks).wait_send()
 
-    routes(0, "wait")
-    routes(1, "wait")
+    def drain_routes(k):
+        for h in range(2):
+            routes(k, h, "wait")
+
+    drain_routes(0)
+    drain_routes(1)
 
     @pl.when(heavy)
     def _():
         for n in range(len(units)):
             drain(n, 2)
-        routes(2, "wait")
+        drain_routes(2)
 
     @pl.when(jnp.logical_not(heavy))
     def _():
@@ -541,7 +580,7 @@
             pltpu.VMEM((NX, VB, 2, CB, 128), F32),
             pltpu.VMEM((3, VB, 2, CB, 128), F32),
             pltpu.VMEM((8, 128), F32),
-            pltpu.VMEM((IJ, 8, 128), F32),
+            pltpu.VMEM((2, 4, 2, 8, 128), F32),
             pltpu.VMEM((256, 512), BF16),
             pltpu.VMEM((ROWS, 3 * QL), BF16),
             pltpu.VMEM((PN, 2 * PC * CB, 3 * QL), BF16),
@@ -552,16 +591,16 @@
             pltpu.VMEM((6, 3, LT, VB, 128), F32),
             pltpu.VMEM((3, LT, VB, 128), F32),
             pltpu.VMEM((128, 128), F32),
-            pltpu.VMEM((3, NX, 72, 128), F32),
-            pltpu.VMEM((16, 72, 128), F32),
+            pltpu.VMEM((3, NX, 2, 40, 128), F32),
+            pltpu.VMEM((16, 2, 40, 128), F32),
             dma((2,)),
             dma((3, 4)), dma((3, 4)),
             dma((3, PN)), dma((3, PN)),
-            dma((15,)), dma((16,)),
+            dma((5,)), dma((5,)),
             dma((9,)), dma((9,)),
             dma((9, 6)), dma((9, 6)),
             dma((9,)), dma((9,)),
-            dma((3, NX, 2)), dma((16,)),
+            dma((3, NX, 2, 2)), dma((16, 2)),
         ],
         compiler_params=pltpu.CompilerParams(
             collective_id=0, has_side_effects=True, vmem_limit_bytes=56 * 1024 * 1024

time: 99.6 us -> 97.2 us (0.976); the launches traced: 98.3 us -> 97 us
  Pallas kernels: 96.5 us -> 95.3 us
    pallas_call x1, Pallas kernels: 96.5 us -> 95.3 us  [local(): pl.pallas_call(ladder, out_shape=jax.ShapeDtypeStruct((slots, 72, 128), F...]
where the time goes in v6:
time: 97.2 us; the launch traced here: 97 us
  Pallas kernels  95.3 us (98%)
  local copies, waits for them, and re-layouts  1.72 us (2%)
    pallas_call x1, Pallas kernels, local(): pl.pallas_call(ladder, out_shape=jax.ShapeDtypeStruct((slots, 72, 128), F...  95.3 us

profile of v6, /device:TPU:64, one launch (start us, length us, event | category | flops | bytes accessed | tf_op | source)
XLA Modules:
  0.0 97.0 jit_solution(15866660047884507884)
XLA Ops:
  0.0 95.3 %shard_map.37 = f32[9,72,128]{2,1,0:T(8,128)} custom-call(s32[1,9]{1,0:T(1,128)} %partners.1, f32[96,2,2,8,128]{4,3,2,1,0:T(8,128)} %bitcast.4, f32[1,64]{1,0:T(1,128)} %amp.1), custom_call_target="tpu_custom_call" | custom-call | tf_op jit(solution)/shard_map/pallas_call | solution.py:570
  95.3 1.7 %copy.7 = f32[9,1,9216]{2,1,0:T(1,128)} copy(f32[9,1,9216]{2,1,0:T(1,128)} %bitcast.5) | data formatting | bytes 663552

commit v7 on v6

--- a/solution.py
+++ b/solution.py
@@ -331,14 +331,14 @@
                 part[k, l, i, a, :] = part[k, l, i, a, :] + ybuf[pair[0], k, l, a, :] + ybuf[pair[1], k, l, a, :]
         z_copy(n, ks).start()
 
-    def routes(k, h, op):
+    def routes(k, h, op, xps=range(NX)):
         if k == 0:
             zk = z
         elif k == 1:
             zk = jnp.where(z == 1, 3, jnp.where(z == 3, 2, 1))
         else:
             zk = jnp.where(z == 0, 3, 0)
-        for xp in range(NX):
+        for xp in xps:
             src = piece.at[k, xp, h]
             valid = jnp.where(gt == 1, xp <= x, xp >= x) if k == 0 else jnp.bool_(True)
             here = xp == x
@@ -354,20 +354,20 @@
                 if op == "start":
                     pltpu.make_async_copy(src, rall.at[p, h], rr.at[p, h]).start()
 
-            @pl.when(jnp.logical_and(valid, jnp.logical_not(here)))
-            def _():
-                send(dev(z, xp, zl, y, core), zk * 4 + x, 0)
-
             if k == 0:
                 @pl.when(valid)
                 def _():
                     keep(z * 4 + xp)
             else:
+                send(dev(zk, x, zl, y, core), z * 4 + xp, 1)
+
                 @pl.when(here)
                 def _():
                     keep(zk * 4 + x)
 
-                send(dev(zk, x, zl, y, core), z * 4 + xp, 1)
+            @pl.when(jnp.logical_and(valid, jnp.logical_not(here)))
+            def _():
+                send(dev(z, xp, zl, y, core), zk * 4 + x, 0)
 
     lane = lax.broadcasted_iota(jnp.int32, (12, 128), 1)
 
@@ -388,7 +388,7 @@
         for xp in range(NX):
             square[0:48] = block(k, xp, h * 48, 48)
             pack(k, xp, h, 0)
-        routes(k, h, "start")
+            routes(k, h, "start", (xp,))
 
     def final_turned(k):
         for xp in range(NX):
@@ -396,8 +396,7 @@
             square[...] = jnp.concatenate([w, jnp.zeros((128 - VB, 128), F32)], axis=0).T
             for h in range(2):
                 pack(k, xp, h, h * 48)
-        for h in range(2):
-            routes(k, h, "start")
+                routes(k, h, "start", (xp,))
 
     def final(k, hs):
         @pl.when(gt == 1)
@@ -476,6 +475,12 @@
                 else:
                     y_step1(n - 1, ks)
                 y_step2(n - 2, ks)
+            if n == 3:
+                @pl.when(ends)
+                def _():
+                    gather(2)
+
+                pump(3)
             stage2(n, ks)
             core_copy(n, ks).start()
             if n > 3:
@@ -484,9 +489,7 @@
                 @pl.when(ends)
                 def _():
                     y_step1(3, ks)
-                    gather(2)
-
-                pump(3)
+
                 behind(2)
             if n == 4:
                 pump(4)
@@ -494,16 +497,16 @@
                 pump(5)
         y_step2(last - 1, ks)
         y_step1(last, ks)
-        for u in (0, 1, 4):
-            z_copy(u, ks).wait_recv()
-        final(0, (0, 1))
         y_step3(last - 2, ks)
         for u in (2, 3, 5):
             z_copy(u, ks).wait_recv()
         for k in range(ks, 0, -1):
             final(k, (0,))
+        y_step2(last, ks)
         y_step3(last - 1, ks)
-        y_step2(last, ks)
+        for u in (0, 1, 4):
+            z_copy(u, ks).wait_recv()
+        final(0, (0, 1))
         y_step3(last, ks)
         for u in (6, 7, 8):
             z_copy(u, ks).wait_recv()

time: 97.2 us -> 97.2 us (level)
  no operation moved by 1% of the time
where the time goes in v7:
time: 97.2 us; the launch traced here: 96.6 us
  Pallas kernels  94.8 us (98%)
  local copies, waits for them, and re-layouts  1.72 us (2%)
    pallas_call x1, Pallas kernels, local(): pl.pallas_call(ladder, out_shape=jax.ShapeDtypeStruct((slots, 72, 128), F...  94.8 us

profile of v7, /device:TPU:64, one launch (start us, length us, event | category | flops | bytes accessed | tf_op | source)
XLA Modules:
  0.0 96.6 jit_solution(619843763112984359)
XLA Ops:
  0.0 94.8 %shard_map.37 = f32[9,72,128]{2,1,0:T(8,128)} custom-call(s32[1,9]{1,0:T(1,128)} %partners.1, f32[96,2,2,8,128]{4,3,2,1,0:T(8,128)} %bitcast.4, f32[1,64]{1,0:T(1,128)} %amp.1), custom_call_target="tpu_custom_call" | custom-call | tf_op jit(solution)/shard_map/pallas_call | solution.py:573
  94.9 1.7 %copy.7 = f32[9,1,9216]{2,1,0:T(1,128)} copy(f32[9,1,9216]{2,1,0:T(1,128)} %bitcast.5) | data formatting | bytes 663552

commit v8 on v7

--- a/solution.py
+++ b/solution.py
@@ -461,8 +461,9 @@
             fetch(ks, m)
         last = len(units) - 1
         for n in range(2, last + 1):
+            if n >= 6:
+                y_step1(n - 1, ks)
             if n == last:
-                y_step1(n - 1, ks)
                 y_step2(n - 2, ks)
             if units[n][0] == "rows":
                 fetch(ks, units[n][1])
@@ -472,7 +473,7 @@
                     @pl.when(jnp.logical_not(ends))
                     def _():
                         y_step1(3, ks)
-                else:
+                elif n < 6:
                     y_step1(n - 1, ks)
                 y_step2(n - 2, ks)
             if n == 3:

time: 97.2 us -> 97.8 us (level)
  Pallas kernels: 94.8 us -> 95.9 us
    pallas_call x1, Pallas kernels: 94.8 us -> 95.9 us  [local(): pl.pallas_call(ladder, out_shape=jax.ShapeDtypeStruct((slots, 72, 128), F...]
where the time goes in v8:
time: 97.8 us; the launch traced here: 97.6 us
  Pallas kernels  95.9 us (98%)
  local copies, waits for them, and re-layouts  1.72 us (2%)
    pallas_call x1, Pallas kernels, local(): pl.pallas_call(ladder, out_shape=jax.ShapeDtypeStruct((slots, 72, 128), F...  95.9 us

profile of v8, /device:TPU:64, one launch (start us, length us, event | category | flops | bytes accessed | tf_op | source)
XLA Modules:
  0.0 97.6 jit_solution(8450257400608727420)
XLA Ops:
  0.0 95.9 %shard_map.37 = f32[9,72,128]{2,1,0:T(8,128)} custom-call(s32[1,9]{1,0:T(1,128)} %partners.1, f32[96,2,2,8,128]{4,3,2,1,0:T(8,128)} %bitcast.4, f32[1,64]{1,0:T(1,128)} %amp.1), custom_call_target="tpu_custom_call" | custom-call | tf_op jit(solution)/shard_map/pallas_call | solution.py:574
  95.9 1.7 %copy.7 = f32[9,1,9216]{2,1,0:T(1,128)} copy(f32[9,1,9216]{2,1,0:T(1,128)} %bitcast.5) | data formatting | bytes 663552
